TPU v7x, 32 devices: a whole 2x2x4 slice. The times are simulated.
32 devices in a mesh: section: 2 (over x), dp: 4 (over y, core), mp: 4 (over z).
Axes of the slice: x: 2, y: 2, z: 4, core: 2. Of those that a mesh axis runs over, the one named last changes fastest.
Arguments:
- hidden: bfloat16 [2, 4, 256, 5120], P('section', 'dp'), may hold values from -6 to 6
- gain: float32 [2, 5120], P('section'), may hold values from 0.5 to 2
- w_first: bfloat16 [2, 5120, 2560], P('section', 'dp', 'mp'), may hold values from -0.078125 to 0.078125
- w_second: bfloat16 [2, 5120, 2560], P('section', 'dp', 'mp'), may hold values from -0.078125 to 0.078125
- lengths: int32 [4, 2], P('dp'), may hold values from 32 to 256, as said below
- cotangent: bfloat16 [2, 4, 256, 5120], P('section', 'dp'), may hold values from -6 to 6
Outputs:
- result: bfloat16 [2, 4, 256, 5120], P('section', 'dp')
- d_hidden: bfloat16 [2, 4, 256, 5120], P('section', 'dp')
- d_gain: float32 [2, 5120], P('section', 'dp')
- d_first: float32 [2, 5120, 2560], P('section', 'dp', 'mp')
- d_second: float32 [2, 5120, 2560], P('section', 'dp', 'mp')
Inputs may be any that keep to these rules, and one draw needn't show every extreme that they name: `lengths`: each row's source count and target count; positions at or past a count are padding.
All inputs are finite; a program needn't handle non-finite values.
Results may differ from a plain program's by a relative error of at most 0.017.
Values may be sent and summed in bfloat16 or wider, within the bound.
No kernel may reach another device: no remote copies, remote signals or barrier semaphores. Data moves between devices by JAX's collectives and lax.ppermute only.
A program may use at most 128 MiB of HBM per device.

v0:
```python
import math

import jax
import jax.numpy as jnp
from jax import lax
from jax.sharding import PartitionSpec as P

HEAD = 128


EPS = 1e-06
MASKED = -1e30


def passed_along(shard, axis, by):
    peers = lax.axis_size(axis)
    pairs = [(i, i + by) for i in range(peers) if 0 <= i + by < peers]
    return lax.ppermute(shard, axis, pairs)


def contract_rows(left, right):
    return lax.dot_general(
        left, right, (((0,), (0,)), ((), ())), preferred_element_type=jnp.float32
    )


def contract_last(left, right):
    return lax.dot_general(
        left, right, (((1,), (1,)), ((), ())), preferred_element_type=jnp.float32
    )


def total_features(partial_value):
    return lax.psum(partial_value, "mp")


def split_heads(values_in):
    batch_size, length, columns = values_in.shape
    return values_in.reshape(batch_size, length, columns // HEAD, HEAD)


def attend(queries, keys, values, key_count):
    batch_size, length, columns = queries.shape
    scale = 1.0 / math.sqrt(HEAD)
    scores = (
        jnp.einsum(
            "bqhd,bkhd->bhqk",
            split_heads(queries),
            split_heads(keys),
            preferred_element_type=jnp.float32,
        )
        * scale
    )
    visible = jnp.arange(length)[None, None, None, :] < key_count[:, None, None, None]
    scores = jnp.where(visible, scores, MASKED)
    weights = jax.nn.softmax(scores, axis=-1)
    weights_low = weights.astype(jnp.bfloat16)
    context = jnp.einsum(
        "bhqk,bkhd->bqhd", weights_low, split_heads(values), preferred_element_type=jnp.float32
    )
    return (context.reshape(batch_size, length, columns).astype(jnp.bfloat16), weights, weights_low)


def attend_back(grad_context, queries, keys, values, weights, weights_low):
    batch_size, length, columns = queries.shape
    scale = 1.0 / math.sqrt(HEAD)
    grad_heads = split_heads(grad_context)
    grad_weights = jnp.einsum(
        "bqhd,bkhd->bhqk", grad_heads, split_heads(values), preferred_element_type=jnp.float32
    )
    grad_values = jnp.einsum(
        "bhqk,bqhd->bkhd", weights_low, grad_heads, preferred_element_type=jnp.float32
    )
    centered = grad_weights - jnp.sum(weights * grad_weights, axis=-1, keepdims=True)
    grad_scores = (weights * centered * scale).astype(jnp.bfloat16)
    grad_queries = jnp.einsum(
        "bhqk,bkhd->bqhd", grad_scores, split_heads(keys), preferred_element_type=jnp.float32
    )
    grad_keys = jnp.einsum(
        "bhqk,bqhd->bkhd", grad_scores, split_heads(queries), preferred_element_type=jnp.float32
    )
    shape_out = (batch_size, length, columns)
    return (
        grad_queries.reshape(shape_out).astype(jnp.bfloat16),
        grad_keys.reshape(shape_out).astype(jnp.bfloat16),
        grad_values.reshape(shape_out).astype(jnp.bfloat16),
    )


def shards(hidden, gain, w_first, w_second, lengths, cotangent):
    encoder = lax.axis_index("section") == 0
    states = hidden[0]
    batch_size, length, width = states.shape
    total_rows = batch_size * length
    gains = gain[0]
    wide = states.astype(jnp.float32)
    inverse = lax.rsqrt(jnp.mean(wide * wide, axis=-1, keepdims=True) + EPS)
    unit = wide * inverse
    normed = (unit * gains).astype(jnp.bfloat16)
    normed_rows = normed.reshape(total_rows, width)
    full_first, full_second = (
        lax.all_gather(w_first[0], "dp", axis=0, tiled=True),
        lax.all_gather(w_second[0], "dp", axis=0, tiled=True),
    )
    columns = full_first.shape[1]
    proj_shape = (batch_size, length, columns)
    first_proj = (
        jnp.dot(normed_rows, full_first, preferred_element_type=jnp.float32)
        .astype(jnp.bfloat16)
        .reshape(proj_shape)
    )

    def values_encoder(operand):
        return (
            jnp.dot(normed_rows, full_second, preferred_element_type=jnp.float32)
            .astype(jnp.bfloat16)
            .reshape(proj_shape)
        )

    def values_decoder(operand):
        return jnp.zeros(proj_shape, jnp.bfloat16)

    second_proj = lax.cond(encoder, values_encoder, values_decoder, 0)
    keys, values = passed_along((first_proj, second_proj), "section", 1)
    heads_here = columns // HEAD
    weight_shape = (batch_size, heads_here, length, length)

    def forward_decoder(operand):
        context, weights, weights_low = attend(first_proj, keys, values, lengths[:, 0])
        out_part = contract_last(context.reshape(total_rows, columns), full_second)
        return (context, weights, weights_low, out_part)

    def forward_encoder(operand):
        return (
            jnp.zeros(proj_shape, jnp.bfloat16),
            jnp.zeros(weight_shape, jnp.float32),
            jnp.zeros(weight_shape, jnp.bfloat16),
            jnp.zeros((total_rows, width), jnp.float32),
        )

    context, weights, weights_low, out_part = lax.cond(encoder, forward_encoder, forward_decoder, 0)
    wide_rows = wide.reshape(total_rows, width)
    unit_rows = unit.reshape(total_rows, width)
    inverse_rows = inverse.reshape(total_rows, 1)
    output_rows = (wide_rows + total_features(out_part)).astype(jnp.bfloat16)
    result = jnp.where(encoder, normed, output_rows.reshape(batch_size, length, width))
    target_keep = jnp.arange(length)[None, :] < lengths[:, 1][:, None]
    grad_out = jnp.where(target_keep[:, :, None], cotangent[0], jnp.zeros((), jnp.bfloat16))
    grad_out_rows = grad_out.reshape(total_rows, width)

    def backward_decoder(operand):
        grad_context = (
            jnp.dot(grad_out_rows, full_second, preferred_element_type=jnp.float32)
            .astype(jnp.bfloat16)
            .reshape(proj_shape)
        )
        return attend_back(grad_context, first_proj, keys, values, weights, weights_low)

    def backward_encoder(operand):
        empty = jnp.zeros(proj_shape, jnp.bfloat16)
        return (empty, empty, empty)

    grad_query, grad_key, grad_value = lax.cond(encoder, backward_encoder, backward_decoder, 0)
    back_key, back_value = passed_along((grad_key, grad_value), "section", -1)
    grad_first = jnp.where(encoder, back_key, grad_query).reshape(total_rows, columns)
    grad_second = jnp.where(encoder, back_value, jnp.zeros((), jnp.bfloat16)).reshape(
        total_rows, columns
    )
    second_left = jnp.where(encoder, normed, grad_out).reshape(total_rows, width)
    second_right = jnp.where(encoder, back_value, context).reshape(total_rows, columns)
    weight_first = contract_rows(normed_rows, grad_first)
    weight_second = contract_rows(second_left, second_right)

    def back_encoder(operand):
        return contract_last(grad_first, full_first) + contract_last(grad_second, full_second)

    def back_decoder(operand):
        return contract_last(grad_first, full_first)

    back_part = lax.cond(encoder, back_encoder, back_decoder, 0)
    extra_rows = jnp.where(encoder, cotangent[0].astype(jnp.float32), 0.0).reshape(
        total_rows, width
    )
    residual_rows = jnp.where(encoder, 0.0, grad_out.astype(jnp.float32)).reshape(total_rows, width)
    grad_normed = total_features(back_part) + extra_rows
    scaled = grad_normed * gains
    inner = jnp.mean(scaled * unit_rows, axis=-1, keepdims=True)
    grad_states = (inverse_rows * (scaled - unit_rows * inner) + residual_rows).astype(jnp.bfloat16)
    gain_part = jnp.sum(grad_normed * unit_rows, axis=0)
    first_sum, second_sum, gain_sum = (
        lax.psum_scatter(
            weight_first.astype(jnp.bfloat16), "dp", scatter_dimension=0, tiled=True
        ).astype(jnp.float32),
        lax.psum_scatter(
            weight_second.astype(jnp.bfloat16), "dp", scatter_dimension=0, tiled=True
        ).astype(jnp.float32),
        lax.psum_scatter(
            gain_part.astype(jnp.bfloat16), "dp", scatter_dimension=0, tiled=True
        ).astype(jnp.float32),
    )
    return (
        result[None],
        grad_states.reshape(batch_size, length, width)[None],
        gain_sum[None],
        first_sum[None],
        second_sum[None],
    )


def solution(mesh):
    return jax.shard_map(
        shards,
        mesh=mesh,
        in_specs=(
            P("section", "dp", None, None),
            P("section", None),
            P("section", "dp", "mp"),
            P("section", "dp", "mp"),
            P("dp", None),
            P("section", "dp", None, None),
        ),
        out_specs=(
            P("section", "dp", None, None),
            P("section", "dp", None, None),
            P("section", "dp"),
            P("section", "dp", "mp"),
            P("section", "dp", "mp"),
        ),
        check_vma=False,
    )
```

profile of v0, /device:TPU:6, one launch (start us, length us, event | category | flops | bytes accessed | tf_op | source)
XLA Modules:
  0.0 684.8 jit_solution(10822728560570049076)
XLA Ops:
  15.2 42.5 %all-gather.5.cloned.1.call-done = bf16[1,5120,640]{2,1,0:T(8,128)(2,1)} async-done(((bf16[1,1280,640]{2,1,0:T(8,128)(2,1)}), bf16[1,5120,640]{2,1,0:T(8,128)(2,1)}) %all-gather.5.cloned.1.call-update) | async-done | bytes 6553616 | tf_op jit(solution)/shard_map/all_gather | solution.py:102
  57.8 5.1 convolution_convert_fusion.8
  64.2 43.0 %all-gather.7.cloned.1.call-done = bf16[1,5120,640]{2,1,0:T(8,128)(2,1)} async-done(((bf16[1,1280,640]{2,1,0:T(8,128)(2,1)}), bf16[1,5120,640]{2,1,0:T(8,128)(2,1)}) %all-gather.7.cloned.1.call-update) | async-done | bytes 6553616 | tf_op jit(solution)/shard_map/all_gather | solution.py:103
  109.5 3.5 bitcast_select_fusion
  112.9 11.1 %collective-permute-done.1 = bf16[1,256,640]{1,2,0:T(8,128)(2,1)} collective-permute-done((bf16[1,256,640]{1,2,0:T(8,128)(2,1)}, bf16[1,256,640]{1,2,0:T(8,128)(2,1)}, u32[]{:S(2)}, u32[]{:S(2)}) %collective-permute-start.1) | collective-permute-done | bytes 327712 | tf_op jit(solution)/shard_map/ppermute | solution.py:18
  124.0 13.9 %conditional.5 = (f32[1,5,256,256]{2,3,1,0:T(8,128)}, bf16[1,5,256,256]{2,3,1,0:T(8,128)(2,1)S(1)}, f32[256,5120]{1,0:T(8,128)}, bf16[1,256,640]{2,1,0:T(8,128)(2,1)}) conditional(s32[]{:T(128)} %convert_element_type.199, (s32[1,2]{1,0:T(1,128)S(1)}, bf16[256,640]{1,0:T(8,128)(2,1)S(1)}, bf16[1,256,640]{2,1,0:T(8,128)(2,1)}, ...), branch_computations={%region_3.6_spmd, %region_6.7_spmd} | conditional | flops 1848279552 | bytes 48840284 | solution.py:141
  131.5 4.5 fusion.60
  137.9 23.3 %conditional.6 = (bf16[1,256,640]{1,2,0:T(8,128)(2,1)}, bf16[1,256,640]{1,2,0:T(8,128)(2,1)}, bf16[1,256,640]{2,1,0:T(8,128)(2,1)S(1)}) conditional(s32[]{:T(128)} %convert_element_type.199, (bf16[256,5120]{1,0:T(8,128)(2,1)}, bf16[5120,640]{1,0:T(8,128)(2,1)}, bf16[1,256,640]{1,2,0:T(8,128)(2,1)}, f32[1,5,256,256]{2,3,1,0:T(8,128)}, ...), branch_computations={%region_8.10_spmd, %region_10.11_spmd} | conditional | flops 2015886080 | bytes 26552400 | solution.py:163
  138.8 6.6 convolution_convert_fusion.5
  167.6 5.2 collective-permute-done.2
  173.6 5.3 collective-permute-done.3
  179.6 7.4 %conditional.7 = (f32[256,5120]{1,0:T(8,128)}) conditional(s32[]{:T(128)} %convert_element_type.199, (bf16[256,640]{1,0:T(8,128)(2,1)S(1)}, bf16[5120,640]{1,0:T(8,128)(2,1)}) %tuple.78, (bf16[256,640]{1,0:T(8,128)(2,1)S(1)}, bf16[5120,640]{1,0:T(8,128)(2,1)}, pred[]{:T(512)}, bf16[1,256,640]{2,1,0:T(8,128)(2,1)S(1)}, ...), branch_computations={%region_11.12_spmd, %region_12.13_spmd} | conditional | flops 3356917760 | bytes 58327132 | solution.py:180
  179.6 7.4 %fusion.58 = f32[256,5120]{1,0:T(8,128)} fusion(bf16[256,640]{1,0:T(8,128)(2,1)S(1)} %get-tuple-element.67, bf16[5120,640]{1,0:T(8,128)(2,1)} %get-tuple-element.68), kind=kOutput, calls=%fused_computation.81 | convolution fusion | flops 1677721600 | bytes 12124160 | tf_op jit(solution)/shard_map/cond/branch_0_fun/dot_general | solution.py:28
  187.1 5.1 convolution_convert_fusion.7
  193.3 7.6 %convolution_convert_fusion.6 = bf16[5120,640]{1,0:T(8,128)(2,1)} fusion(bf16[1,1,256,5120]{3,2,1,0:T(8,128)(2,1)} %param.19, pred[256]{0:T(512)(128)(4,1)S(1)} %iota_compare_fusion.1, pred[]{:T(512)} %eq.3, bf16[1,1,256,5120]{3,2,1,0:T(8,128)(2,1)S(1)} %copy-done, f32[5120]{0:T(1024)S(1)} %bitcast.184, f32[256]{0:T(256)S(1)} %add_rsqrt_fusion, ...), kind=kOutput, calls=%fused_computation.33 | convolution fusion | flops 1689026560 | bytes 12473601 | tf_op jit(solution)/shard_map/dot_general | solution.py:22
  202.8 348.8 %all-reduce.4.cloned.1.call-done = (f32[256,5120]{1,0:T(8,128)}, f32[256,5120]{1,0:T(8,128)}) async-done(((f32[256,5120]{1,0:T(8,128)}, f32[256,5120]{1,0:T(8,128)}), (f32[256,5120]{1,0:T(8,128)}, f32[256,5120]{1,0:T(8,128)})) %all-reduce.4.cloned.1.call-update) | async-done | bytes 10485776 | tf_op jit(solution)/shard_map/psum | solution.py:34
  551.6 5.4 fusion.34
  557.0 10.2 %all-reduce = bf16[5120]{0:T(1024)(128)(2,1)S(1)} all-reduce(bf16[5120]{0:T(1024)(128)(2,1)S(1)} %get-tuple-element.131), channel_id=4, replica_groups=mesh['section'=2,'dp'=4,'mp'=4] {'dp'}, use_global_device_ids=true, to_apply=%region_16.17.clone | all-reduce | flops 5120 | bytes 20480
  567.9 5.3 fusion.40
  573.2 3.8 fusion.41
  577.0 35.2 %reduce-scatter.3.cloned.1.call-done = bf16[1280,640]{1,0:T(8,128)(2,1)} async-done(((bf16[5120,640]{1,0:T(8,128)(2,1)}), bf16[1280,640]{1,0:T(8,128)(2,1)}) %reduce-scatter.3.cloned.1.call-update) | async-done | bytes 1638416 | tf_op jit(solution)/shard_map/reduce_scatter | solution.py:191
  612.2 3.3 bitcast_convert_fusion.1
  615.5 59.3 %reduce-scatter.5.cloned.1.call-done = bf16[1280,640]{1,0:T(8,128)(2,1)} async-done(((bf16[5120,640]{1,0:T(8,128)(2,1)}), bf16[1280,640]{1,0:T(8,128)(2,1)}) %reduce-scatter.5.cloned.1.call-update) | async-done | bytes 1638416 | tf_op jit(solution)/shard_map/reduce_scatter | solution.py:194
  674.9 3.3 bitcast_convert_fusion
  (76 shorter events, 48.4 us)
Async XLA Ops:
  7.2 5.8 copy-start
  7.2 5.8 copy-start.9
  7.2 50.6 %all-gather.5.cloned.1.call-start = ((), (), s32[]{:S(2)}) async-start(), calls=%async_computation.4 | async-start | bytes 8192000 | tf_op jit(solution)/shard_map/all_gather | solution.py:102
  7.9 99.3 %all-gather.7.cloned.1.call-start = ((), (), s32[]{:S(2)}) async-start(), calls=%async_computation.5 | async-start | bytes 8192000 | tf_op jit(solution)/shard_map/all_gather | solution.py:103
  8.7 542.9 %all-reduce.4.cloned.1.call-start = ((), (), s32[]{:S(2)}) async-start(), calls=%async_computation.6 | async-start | bytes 20971520 | tf_op jit(solution)/shard_map/psum | solution.py:34
  62.9 61.2 %copy-start.8 = (bf16[256,640]{1,0:T(8,128)(2,1)}, bf16[256,640]{1,0:T(8,128)(2,1)S(1)}, u32[]{:S(2)}) copy-start(bf16[256,640]{1,0:T(8,128)(2,1)S(1)} %convolution_convert_fusion.8) | copy-start | bytes 983044
  62.9 50.1 %collective-permute-start = (bf16[1,256,640]{2,1,0:T(8,128)(2,1)S(1)}, bf16[1,256,640]{2,1,0:T(8,128)(2,1)}, u32[]{:S(2)}, u32[]{:S(2)}) collective-permute-start(bf16[1,256,640]{2,1,0:T(8,128)(2,1)S(1)} %bitcast.180), channel_id=1, source_target_pairs={{0,16},{1,17},{2,18},{3,19},{4,20},{5,21},{6,22},{7,23},{8,24},{9,... | collective-permute-start | bytes 983048 | tf_op jit(solution)/shard_map/ppermute | solution.py:18
  107.3 16.8 %copy-start.16 = (s32[1,2]{1,0:T(1,128)S(1)}, s32[1,2]{1,0:T(1,128)}, u32[]{:S(2)}) copy-start(s32[1,2]{1,0:T(1,128)} %param.18) | copy-start | bytes 28
  108.2 15.9 %collective-permute-start.1 = (bf16[1,256,640]{1,2,0:T(8,128)(2,1)}, bf16[1,256,640]{1,2,0:T(8,128)(2,1)}, u32[]{:S(2)}, u32[]{:S(2)}) collective-permute-start(bf16[1,256,640]{1,2,0:T(8,128)(2,1)} %copy.53), channel_id=1, source_target_pairs={{0,16},{1,17},{2,18},{3,19},{4,20},{5,21},{6,22},{7,23},{8,24},{9,... | collective-permute-start | bytes 983048 | tf_op jit(solution)/shard_map/ppermute | solution.py:18
  127.1 4.4 copy-start.1
  131.5 4.6 copy-start.7
  137.9 0.8 copy-start.6
  146.5 1.9 copy-start.5
  163.1 9.7 %collective-permute-start.2 = (bf16[1,256,640]{2,1,0:T(8,128)(2,1)}, bf16[1,256,640]{2,1,0:T(8,128)(2,1)S(1)}, u32[]{:S(2)}, u32[]{:S(2)}) collective-permute-start(bf16[1,256,640]{2,1,0:T(8,128)(2,1)} %copy.59), channel_id=1, source_target_pairs={{16,0},{17,1},{18,2},{19,3},{20,4},{21,5},{22,6},{23,7},{24,8},{25... | collective-permute-start | bytes 983048 | tf_op jit(solution)/shard_map/ppermute | solution.py:18
  166.3 12.6 %collective-permute-start.3 = (bf16[1,256,640]{2,1,0:T(8,128)(2,1)}, bf16[1,256,640]{2,1,0:T(8,128)(2,1)S(1)}, u32[]{:S(2)}, u32[]{:S(2)}) collective-permute-start(bf16[1,256,640]{2,1,0:T(8,128)(2,1)} %copy.61), channel_id=1, source_target_pairs={{16,0},{17,1},{18,2},{19,3},{20,4},{21,5},{22,6},{23,7},{24,8},{25... | collective-permute-start | bytes 983048 | tf_op jit(solution)/shard_map/ppermute | solution.py:18
  172.8 0.7 copy-start.10
  178.9 0.7 copy-start.12
  187.1 425.1 %reduce-scatter.3.cloned.1.call-start = ((), (), s32[]{:S(2)}) async-start(), calls=%async_computation.2 | async-start | bytes 8192000 | tf_op jit(solution)/shard_map/reduce_scatter | solution.py:191
  192.2 1.0 copy-start.11
  192.2 1.1 copy-start.13
  192.3 482.6 %reduce-scatter.5.cloned.1.call-start = ((), (), s32[]{:S(2)}) async-start(), calls=%async_computation.3 | async-start | bytes 8192000 | tf_op jit(solution)/shard_map/reduce_scatter | solution.py:194
  200.9 0.7 copy-start.17
  567.9 5.3 copy-start.3
  567.9 5.3 copy-start.4
Sparse Core Ops, SparseCore 0:
  9.6 48.1 all-gather.4
  59.3 47.8 all-gather.6
  187.2 364.3 all-reduce.3
  554.0 58.1 reduce-scatter.2
  614.7 60.0 reduce-scatter.4
where the time goes:
time: 688 us; the launch traced here: 685 us
  waiting for transfers between devices  552 us (80%)
  matrix products  48 us (7%)
  other arithmetic  34.3 us (5%)
  local copies, waits for them, and re-layouts  20.1 us (3%)
  between operations  14.6 us (2%)
  blocking collectives  10.2 us (1%)
    psum x1, waiting for transfers between devices, total_features(): return lax.psum(partial_value, 'mp')  349 us
    reduce_scatter x1, waiting for transfers between devices, shards(): lax.psum_scatter(weight_second.astype(jnp.bfloat16), 'dp', scatter_dimens...  59.3 us
    all_gather x1, waiting for transfers between devices, shards(): lax.all_gather(w_second[0], 'dp', axis=0, tiled=True)  43 us
    all_gather x1, waiting for transfers between devices, shards(): lax.all_gather(w_first[0], 'dp', axis=0, tiled=True)  42.5 us
    reduce_scatter x1, waiting for transfers between devices, shards(): lax.psum_scatter(weight_first.astype(jnp.bfloat16), 'dp', scatter_dimensi...  35.2 us
    ppermute x4, waiting for transfers between devices, passed_along(): return lax.ppermute(shard, axis, pairs)  21.6 us
  transfers between devices with their start and end apart: 9, of which 8 were waited for; matrix products, arithmetic and copies ran while one was open for 7% of the time, Pallas kernels for 0%

commit v1 on v0

v1 whole, which is shorter than its diff:
```python
import math

import jax
import jax.numpy as jnp
from jax import lax
from jax.experimental import pallas as pl
from jax.experimental.pallas import tpu as pltpu
from jax.sharding import PartitionSpec as P

HEAD = 128
EPS = 1e-06
MASKED = -1e30
CORES = 2
F32 = jnp.float32
BF16 = jnp.bfloat16


def dot_rows(left, right):
    return lax.dot_general(left, right, (((0,), (0,)), ((), ())), preferred_element_type=F32)


def dot_last(left, right):
    return lax.dot_general(left, right, (((1,), (1,)), ((), ())), preferred_element_type=F32)


def dot_plain(left, right):
    return jnp.dot(left, right, preferred_element_type=F32)


def core_swap(x):
    n = lax.axis_size("dp")
    return lax.ppermute(x, "dp", [(i, i ^ 1) for i in range(n)])


def chip_shift(x, by, decoder_only=False):
    n = lax.axis_size("dp")
    to = [(i + by * CORES) % n for i in range(n)]
    if decoder_only:
        return lax.ppermute(x, ("section", "dp"), [(n + i, n + to[i]) for i in range(n)])
    return lax.ppermute(x, "dp", [(i, to[i]) for i in range(n)])


def head_shift(x, by, decoder_only=False):
    n = lax.axis_size("mp")
    pairs = [(i, (i + by) % n) for i in range(n)]
    if decoder_only:
        return lax.ppermute(x, ("section", "mp"), [(n + i, n + t) for i, t in pairs])
    return lax.ppermute(x, "mp", pairs)


def attention_kernel(lengths_ref, q_ref, k_ref, v_ref, g_ref, ctx_ref, gq_ref, gk_ref, gv_ref):
    scale = 1.0 / math.sqrt(HEAD)
    q, k, v, g = q_ref[...], k_ref[...], v_ref[...], g_ref[...]
    scores = dot_last(q, k) * scale
    column = lax.broadcasted_iota(jnp.int32, scores.shape, 1)
    scores = jnp.where(column < lengths_ref[0, 0], scores, MASKED)
    top = jnp.max(scores, axis=-1, keepdims=True)
    raised = jnp.exp(scores - top)
    weights = raised / jnp.sum(raised, axis=-1, keepdims=True)
    low = weights.astype(BF16)
    ctx_ref[...] = dot_plain(low, v).astype(BF16)
    gv_ref[...] = dot_rows(low, g).astype(BF16)
    grad_weights = dot_last(g, v)
    centered = grad_weights - jnp.sum(weights * grad_weights, axis=-1, keepdims=True)
    grad_scores = (weights * centered * scale).astype(BF16)
    gq_ref[...] = dot_plain(grad_scores, k).astype(BF16)
    gk_ref[...] = dot_rows(grad_scores, q).astype(BF16)


def attention(lengths, q, k, v, g):
    rows, columns = q.shape
    block = pl.BlockSpec((rows, HEAD), lambda h: (0, h))
    shape = jax.ShapeDtypeStruct((rows, columns), BF16)
    heads = columns // HEAD
    return pl.pallas_call(
        attention_kernel,
        grid=(heads,),
        in_specs=[pl.BlockSpec(memory_space=pltpu.SMEM)] + [block] * 4,
        out_specs=[block] * 4,
        out_shape=[shape] * 4,
        compiler_params=pltpu.CompilerParams(vmem_limit_bytes=32 * 2**20),
        cost_estimate=pl.CostEstimate(
            flops=14 * rows * rows * columns,
            bytes_accessed=16 * rows * columns,
            transcendentals=heads * rows * rows,
        ),
        name="attention",
    )(lengths, q, k, v, g)


def ring_sum(parts, me, decoder_only):
    n = parts.shape[1]

    def block(i):
        return lax.dynamic_index_in_dim(parts, lax.rem(i, n), 1, False)

    total = block(me + n - 1)
    for step in range(n - 1):
        total = head_shift(total, 1, decoder_only)
        mine = block(me + 2 * n - 2 - step)
        total = total.astype(F32) + mine.astype(F32)
        if step < n - 2:
            total = total.astype(BF16)
    return total


def ring_gather(rows, me, n, decoder_only):
    whole = jnp.zeros((n,) + rows.shape, rows.dtype)
    whole = lax.dynamic_update_index_in_dim(whole, rows, me, 0)
    held = rows
    for step in range(1, n):
        held = head_shift(held, 1, decoder_only)
        whole = lax.dynamic_update_index_in_dim(whole, held, lax.rem(me + n - step, n), 0)
    return whole.reshape(n * rows.shape[0], rows.shape[1])


def shards(hidden, gain, w_first, w_second, lengths, cotangent):
    encoder = lax.axis_index("section") == 0
    place = lax.axis_index("dp")
    chip, core = place // CORES, lax.rem(place, CORES)
    head_place = lax.axis_index("mp")
    heads_axis = lax.axis_size("mp")
    chips = lax.axis_size("dp") // CORES
    states = hidden[0, 0]
    length, width = states.shape
    gains = gain[0][None, :]
    span = width // chips
    tile = w_first.shape[1]
    columns = w_first.shape[2]
    block = length // heads_axis

    def chip_at(k):
        return lax.rem(chip + k, chips)

    def chip_columns(array, k):
        return lax.dynamic_slice_in_dim(array, chip_at(k) * span, span, 1)

    first, second = w_first[0], w_second[0]

    def whole_chip(own):
        other = core_swap(own)
        return jnp.concatenate(
            [jnp.where(core == 0, own, other), jnp.where(core == 0, other, own)], axis=0
        )

    wide = states.astype(F32)
    inverse = lax.rsqrt(jnp.mean(wide * wide, axis=-1, keepdims=True) + EPS)
    unit = wide * inverse
    normed = (unit * gains).astype(BF16)
    keep = jnp.arange(length)[:, None] < lengths[0, 1]
    grad_out = jnp.where(keep, cotangent[0, 0], jnp.zeros((), BF16))

    left = [chip_columns(normed, 0)]
    left += [chip_shift(chip_columns(normed, k), k) for k in range(1, chips)]
    upper = [chip_columns(grad_out, 0)]
    upper += [chip_shift(chip_columns(grad_out, k), k, True) for k in range(1, chips)]
    first_chip = whole_chip(first)
    second_chip = whole_chip(second)
    right = [jnp.where(encoder, left[k], upper[k]) for k in range(chips)]

    def project(rows, weight):
        parts = [dot_plain(rows[k], weight) for k in range(chips)]
        total = parts[0]
        for k in range(1, chips):
            total = total + chip_shift(parts[k].astype(BF16), -k).astype(F32)
        return total.astype(BF16)

    first_proj = project(left, first_chip)
    second_proj = project(right, second_chip)
    keys = lax.ppermute(first_proj, "section", [(0, 1)])
    values = lax.ppermute(second_proj, "section", [(0, 1)])
    context, grad_query, grad_key, grad_value = attention(
        lengths, first_proj, keys, values, second_proj
    )
    back_value = lax.ppermute(grad_value, "section", [(1, 0)])
    back_key = lax.ppermute(grad_key, "section", [(1, 0)])
    grad_second = jnp.where(encoder, back_value, context)
    grad_first = jnp.where(encoder, back_key, grad_query)
    grads_second = [grad_second] + [chip_shift(grad_second, k) for k in range(1, chips)]
    grads_first = [grad_first] + [chip_shift(grad_first, k) for k in range(1, chips)]

    split = (chips, heads_axis, block, span)
    part_second = jnp.stack([dot_last(g, second_chip) for g in grads_second])
    part_first = jnp.stack([dot_last(g, first_chip) for g in grads_first])
    out_parts = part_second.astype(BF16).reshape(split)
    back_parts = (part_first + jnp.where(encoder, part_second, 0.0)).astype(BF16).reshape(split)

    def full_rows(sums, decoder_only):
        whole = jnp.zeros((block, width), F32)
        whole = lax.dynamic_update_slice_in_dim(whole, sums[0], chip * span, 1)
        for k in range(1, chips):
            got = chip_shift(sums[k].astype(BF16), -k, decoder_only).astype(F32)
            whole = lax.dynamic_update_slice_in_dim(whole, got, chip_at(k) * span, 1)
        return whole

    def my_rows(array):
        return lax.dynamic_slice_in_dim(array, head_place * block, block, 0)

    out_rows = full_rows(ring_sum(out_parts, head_place, True), True)
    out_rows = (my_rows(states).astype(F32) + out_rows).astype(BF16)
    output = ring_gather(out_rows, head_place, heads_axis, True)
    result = jnp.where(encoder, normed, output)

    grad_normed = full_rows(ring_sum(back_parts, head_place, False), False)
    grad_normed = grad_normed + jnp.where(encoder, my_rows(cotangent[0, 0]).astype(F32), 0.0)
    my_inverse = my_rows(inverse)
    my_unit = my_rows(states).astype(F32) * my_inverse
    residual = jnp.where(encoder, 0.0, my_rows(grad_out).astype(F32))
    scaled = grad_normed * gains
    inner = jnp.mean(scaled * my_unit, axis=-1, keepdims=True)
    grad_rows = (my_inverse * (scaled - my_unit * inner) + residual).astype(BF16)
    grad_states = ring_gather(grad_rows, head_place, heads_axis, False)

    gain_part = jnp.sum(grad_normed * my_unit, axis=0, keepdims=True)
    gain_chip = chip_columns(gain_part, 0)
    for k in range(1, chips):
        gain_chip = gain_chip + chip_shift(chip_columns(gain_part, k), k)
    gain_mine = lax.dynamic_slice_in_dim(gain_chip, core * tile, tile, 1)
    gain_mine = gain_mine + core_swap(
        lax.dynamic_slice_in_dim(gain_chip, (1 - core) * tile, tile, 1)
    )
    gain_sum = gain_mine
    for k in range(1, heads_axis):
        gain_sum = gain_sum + head_shift(gain_mine, k)

    def weight_grad(rows, grads):
        rows, grads = jnp.concatenate(rows, axis=0), jnp.concatenate(grads, axis=0)
        own = dot_rows(lax.dynamic_slice_in_dim(rows, core * tile, tile, 1), grads)
        other = dot_rows(lax.dynamic_slice_in_dim(rows, (1 - core) * tile, tile, 1), grads)
        return own + core_swap(other.astype(BF16)).astype(F32)

    first_sum = weight_grad(left, grads_first)
    second_sum = weight_grad(right, grads_second)
    return (
        result[None, None],
        grad_states[None, None],
        gain_sum,
        first_sum[None],
        second_sum[None],
    )


def solution(mesh):
    return jax.shard_map(
        shards,
        mesh=mesh,
        in_specs=(
            P("section", "dp", None, None),
            P("section", None),
            P("section", "dp", "mp"),
            P("section", "dp", "mp"),
            P("dp", None),
            P("section", "dp", None, None),
        ),
        out_specs=(
            P("section", "dp", None, None),
            P("section", "dp", None, None),
            P("section", "dp"),
            P("section", "dp", "mp"),
            P("section", "dp", "mp"),
        ),
        check_vma=False,
    )
```

time: 688 us -> 342 us (0.50)
  waiting for transfers between devices: 552 us -> 191 us
  starting transfers between devices: 5.59 us -> 90 us
  matrix products: 48 us -> 24.1 us
  local copies, waits for them, and re-layouts: 20.1 us -> 4.93 us
  between operations: 14.6 us -> 1.54 us
  other arithmetic: 34.3 us -> 21.3 us
  blocking collectives: 10.2 us -> 0 us
    psum x1 -> x0, waiting for transfers between devices: 349 us -> none  [total_features(): return lax.psum(partial_value, 'mp')]
    ppermute x4 -> x33, waiting for transfers between devices: 21.6 us -> 191 us  [the longest x9 51.8 us: head_shift(): return lax.ppermute(x, 'mp', pairs)]
    reduce_scatter x2 -> x0, waiting for transfers between devices: 94.5 us -> none  [the longest x1 59.3 us: shards(): lax.psum_scatter(weight_second.astype(jnp.bfloat16), 'dp', scatter_dimens...]
    all_gather x2 -> x0, waiting for transfers between devices: 85.5 us -> none  [the longest x1 43 us: shards(): lax.all_gather(w_second[0], 'dp', axis=0, tiled=True)]
    ppermute x4 -> x33, starting transfers between devices: 5.17 us -> 90 us  [the longest x9 54.3 us: head_shift(): return lax.ppermute(x, 'mp', pairs)]
    dot_general x11 -> x12, matrix products: 46.4 us -> 24.1 us  [the longest x4 10.5 us: dot_rows(): lax.dot_general(left, right, (((0,), (0,)), ((), ())), preferred_element_...]
    broadcast_in_dim x4 -> x0, other arithmetic: 12.1 us -> none  [the longest x1 5.28 us: shards(): result[None]]
    unnamed x1 -> x0, blocking collectives: 10.2 us -> none
  transfers between devices with their start and end apart: 9 -> 33, of which waited for: 8 -> 23; matrix products, arithmetic and copies ran while one was open for 7% -> 12% of each run, Pallas kernels for 0% -> 0%
where the time goes in v1:
time: 342 us; the launch traced here: 338 us
  waiting for transfers between devices  191 us (56%)
  starting transfers between devices  90 us (26%)
  matrix products  24.1 us (7%)
  other arithmetic  21.3 us (6%)
  local copies, waits for them, and re-layouts  4.93 us (1%)
  Pallas kernels  4.9 us (1%)
    ppermute x9, starting transfers between devices, head_shift(): return lax.ppermute(x, 'mp', pairs)  54.3 us
    ppermute x9, waiting for transfers between devices, head_shift(): return lax.ppermute(x, 'mp', pairs)  51.8 us
    ppermute x7, waiting for transfers between devices, chip_shift(): return lax.ppermute(x, 'dp', [(i, to[i]) for i in range(n)])  51.3 us
    ppermute x6, waiting for transfers between devices, head_shift(): lax.ppermute(x, ('section', 'mp'), [(n + i, n + t) for i, t in pairs])  44.6 us
    ppermute x2, waiting for transfers between devices, chip_shift(): lax.ppermute(x, ('section', 'dp'), [(n + i, n + to[i]) for i in range(n)])  26.9 us
    ppermute x6, starting transfers between devices, head_shift(): lax.ppermute(x, ('section', 'mp'), [(n + i, n + t) for i, t in pairs])  19.1 us
    dot_general x4, matrix products, dot_rows(): lax.dot_general(left, right, (((0,), (0,)), ((), ())), preferred_element_...  10.5 us
    ppermute x1, waiting for transfers between devices, shards(): keys = lax.ppermute(first_proj, 'section', [(0, 1)])  7.52 us
  transfers between devices with their start and end apart: 33, of which 23 were waited for; matrix products, arithmetic and copies ran while one was open for 12% of the time, Pallas kernels for 0%

profile of v1, /device:TPU:6, one launch (start us, length us, event | category | flops | bytes accessed | tf_op | source)
XLA Modules:
  0.0 337.8 jit_solution(1550387134552162257)
XLA Ops:
  10.1 3.4 %collective-permute-start.5 = (bf16[256,2560]{1,0:T(8,128)(2,1)}, bf16[256,2560]{1,0:T(8,128)(2,1)}, u32[]{:S(2)}, u32[]{:S(2)}) collective-permute-start(bf16[256,2560]{1,0:T(8,128)(2,1)} %get-tuple-element.25), channel_id=1, source_target_pairs={{16,24},{20,28},{24,16},{28,20},{17,25},{21,29},{25,17},{29,21},{1... | collective-permute-start | bytes 3932168 | tf_op jit(solution)/shard_map/ppermute | solution.py:39
  14.1 27.5 %collective-permute-done.1 = bf16[256,2560]{1,0:T(8,128)(2,1)} collective-permute-done((bf16[256,2560]{1,0:T(8,128)(2,1)}, bf16[256,2560]{1,0:T(8,128)(2,1)}, u32[]{:S(2)}, u32[]{:S(2)}) %collective-permute-start.1) | collective-permute-done | bytes 1310752 | tf_op jit(solution)/shard_map/ppermute | solution.py:40
  41.6 26.9 %collective-permute-done.5 = bf16[256,2560]{1,0:T(8,128)(2,1)} collective-permute-done((bf16[256,2560]{1,0:T(8,128)(2,1)}, bf16[256,2560]{1,0:T(8,128)(2,1)}, u32[]{:S(2)}, u32[]{:S(2)}) %collective-permute-start.5) | collective-permute-done | bytes 1310752 | tf_op jit(solution)/shard_map/ppermute | solution.py:39
  76.3 3.6 %convolution_convert_fusion.3 = bf16[256,640]{1,0:T(8,128)(2,1)S(1)} fusion(bf16[256,2560]{1,0:T(8,128)(2,1)} %collective-permute-done.1, bf16[1280,640]{1,0:T(8,128)(2,1)S(1)} %get-tuple-element.24, bf16[1280,640]{1,0:T(8,128)(2,1)S(1)} %get-tuple-element.23), kind=kOutput, calls=%fused_computation.67 | convolution fusion | flops 845578240 | bytes 4915200 | tf_op jit(solution)/shard_map/dot_general | solution.py:27
  85.5 3.7 %collective-permute-done.2 = bf16[256,640]{1,0:T(8,128)(2,1)S(1)} collective-permute-done((bf16[256,640]{1,0:T(8,128)(2,1)S(1)}, bf16[256,640]{1,0:T(8,128)(2,1)S(1)}, u32[]{:S(2)}, u32[]{:S(2)}) %collective-permute-start.2) | collective-permute-done | bytes 327712 | tf_op jit(solution)/shard_map/ppermute | solution.py:40
  93.1 7.5 %collective-permute-done.3.k_ref = bf16[256,640]{1,0:T(8,128)(2,1)S(1)} collective-permute-done((bf16[256,640]{1,0:T(8,128)(2,1)S(1)}, bf16[256,640]{1,0:T(8,128)(2,1)S(1)}, u32[]{:S(2)}, u32[]{:S(2)}) %collective-permute-start.3) | collective-permute-done | bytes 327712 | tf_op jit(solution)/shard_map/ppermute | solution.py:170
  100.6 4.9 %attention.1 = (bf16[256,640]{1,0:T(8,128)(2,1)S(1)}, bf16[256,640]{1,0:T(8,128)(2,1)S(1)}, bf16[256,640]{1,0:T(8,128)(2,1)S(1)}, bf16[256,640]{1,0:T(8,128)(2,1)S(1)}) custom-call(s32[1,2]{1,0:T(1,128)S(1)} %copy-done, bf16[256,640]{1,0:T(8,128)(2,1)S(1)} %fusion.34.q_ref, bf16[256,640]{1,0:T(8,128)(2,1)S(1)} %collective-permute-done.3.k_ref, ...), custom_call_target="tpu_custom_call" | custom-call | flops 587202560 | bytes 2621440 | tf_op jit(solution)/shard_map/attention/pallas_call | solution.py:75
  108.6 6.5 %collective-permute-done.8 = bf16[256,640]{1,0:T(8,128)(2,1)S(1)} collective-permute-done((bf16[256,640]{1,0:T(8,128)(2,1)S(1)}, bf16[256,640]{1,0:T(8,128)(2,1)S(1)}, u32[]{:S(2)}, u32[]{:S(2)}) %collective-permute-start.8) | collective-permute-done | bytes 327712 | tf_op jit(solution)/shard_map/ppermute | solution.py:175
  121.4 4.3 %collective-permute-done.9 = bf16[256,640]{1,0:T(8,128)(2,1)S(1)} collective-permute-done((bf16[256,640]{1,0:T(8,128)(2,1)S(1)}, bf16[256,640]{1,0:T(8,128)(2,1)S(1)}, u32[]{:S(2)}, u32[]{:S(2)}) %collective-permute-start.9) | collective-permute-done | bytes 327712 | tf_op jit(solution)/shard_map/ppermute | solution.py:40
  133.2 3.5 %collective-permute-start.10 = (bf16[2,64,2560]{2,1,0:T(8,128)(2,1)S(1)}, bf16[2,64,2560]{2,1,0:T(8,128)(2,1)S(1)}, u32[]{:S(2)}, u32[]{:S(2)}) collective-permute-start(bf16[2,64,2560]{2,1,0:T(8,128)(2,1)S(1)} %dynamic-slice_bitcast_fusion.1), channel_id=1, source_target_pairs={{16,17},{17,18},{18,19},{19,16},{20,21},{21,22},{22,23},{23,20},{2... | collective-permute-start | bytes 1966088 | tf_op jit(solution)/shard_map/ppermute | solution.py:47
  140.6 13.8 %collective-permute-done.10 = bf16[2,64,2560]{2,1,0:T(8,128)(2,1)S(1)} collective-permute-done((bf16[2,64,2560]{2,1,0:T(8,128)(2,1)S(1)}, bf16[2,64,2560]{2,1,0:T(8,128)(2,1)S(1)}, u32[]{:S(2)}, u32[]{:S(2)}) %collective-permute-start.10) | collective-permute-done | bytes 655392 | tf_op jit(solution)/shard_map/ppermute | solution.py:47
  156.5 11.9 %collective-permute-done.19 = bf16[2,64,2560]{2,1,0:T(8,128)(2,1)S(1)} collective-permute-done((bf16[2,64,2560]{2,1,0:T(8,128)(2,1)S(1)}, bf16[2,64,2560]{2,1,0:T(8,128)(2,1)S(1)}, u32[]{:S(2)}, u32[]{:S(2)}) %collective-permute-start.19) | collective-permute-done | bytes 655392 | tf_op jit(solution)/shard_map/ppermute | solution.py:48
  168.7 13.8 %collective-permute-done.11 = bf16[2,64,2560]{2,1,0:T(8,128)(2,1)S(1)} collective-permute-done((bf16[2,64,2560]{2,1,0:T(8,128)(2,1)S(1)}, bf16[2,64,2560]{2,1,0:T(8,128)(2,1)S(1)}, u32[]{:S(2)}, u32[]{:S(2)}) %collective-permute-start.11) | collective-permute-done | bytes 655392 | tf_op jit(solution)/shard_map/ppermute | solution.py:47
  184.6 11.9 %collective-permute-done.20 = bf16[2,64,2560]{2,1,0:T(8,128)(2,1)S(1)} collective-permute-done((bf16[2,64,2560]{2,1,0:T(8,128)(2,1)S(1)}, bf16[2,64,2560]{2,1,0:T(8,128)(2,1)S(1)}, u32[]{:S(2)}, u32[]{:S(2)}) %collective-permute-start.20) | collective-permute-done | bytes 655392 | tf_op jit(solution)/shard_map/ppermute | solution.py:48
  199.7 4.0 %fusion.9 = f32[1,1280,640]{2,1,0:T(8,128)} fusion(bf16[1280,640]{1,0:T(8,128)(2,1)S(1)} %collective-permute-done.31, s32[]{:T(128)S(6)} %select_n.188, bf16[256,2560]{1,0:T(8,128)(2,1)S(1)} %copy-done.19, bf16[256,2560]{1,0:T(8,128)(2,1)} %collective-permute-done.1, bf16[256,640]{1,0:T(8,128)(2,1)S(1)} %collective-permute-done.18, ...), kind=kOutput, calls=%fused_computation.15 | convolution fusion | flops 844431360 | bytes 8192004 | tf_op jit(solution)/shard_map/dot_general | solution.py:19
  203.8 6.8 %collective-permute-done.12 = bf16[2,64,2560]{2,1,0:T(8,128)(2,1)S(1)} collective-permute-done((bf16[2,64,2560]{2,1,0:T(8,128)(2,1)S(1)}, bf16[2,64,2560]{2,1,0:T(8,128)(2,1)S(1)}, u32[]{:S(2)}, u32[]{:S(2)}) %collective-permute-start.12) | collective-permute-done | bytes 655392 | tf_op jit(solution)/shard_map/ppermute | solution.py:47
  213.2 11.1 %collective-permute-done.21 = bf16[2,64,2560]{2,1,0:T(8,128)(2,1)S(1)} collective-permute-done((bf16[2,64,2560]{2,1,0:T(8,128)(2,1)S(1)}, bf16[2,64,2560]{2,1,0:T(8,128)(2,1)S(1)}, u32[]{:S(2)}, u32[]{:S(2)}) %collective-permute-start.21) | collective-permute-done | bytes 655392 | tf_op jit(solution)/shard_map/ppermute | solution.py:48
  225.1 8.8 %collective-permute-done.22 = bf16[64,2560]{1,0:T(8,128)(2,1)S(1)} collective-permute-done((bf16[64,2560]{1,0:T(8,128)(2,1)S(1)}, bf16[64,2560]{1,0:T(8,128)(2,1)S(1)}, u32[]{:S(2)}, u32[]{:S(2)}) %collective-permute-start.22) | collective-permute-done | bytes 327712 | tf_op jit(solution)/shard_map/ppermute | solution.py:40
  249.6 10.6 %collective-permute-done.28 = f32[1,1280]{1,0:T(1,128)S(1)} collective-permute-done((f32[1,1280]{1,0:T(1,128)S(1)}, f32[1,1280]{1,0:T(1,128)S(1)}, u32[]{:S(2)}, u32[]{:S(2)}) %collective-permute-start.28) | collective-permute-done | bytes 5152 | tf_op jit(solution)/shard_map/ppermute | solution.py:48
  261.0 42.5 %collective-permute-start.24 = (bf16[64,5120]{1,0:T(8,128)(2,1)S(1)}, bf16[64,5120]{1,0:T(8,128)(2,1)S(1)}, u32[]{:S(2)}, u32[]{:S(2)}) collective-permute-start(bf16[64,5120]{1,0:T(8,128)(2,1)S(1)} %collective-permute-done.23), channel_id=1, source_target_pairs={{0,1},{1,2},{2,3},{3,0},{4,5},{5,6},{6,7},{7,4},{8,9},{9,10},{10,1... | collective-permute-start | bytes 1966088 | tf_op jit(solution)/shard_map/ppermute | solution.py:48
  305.5 6.0 %collective-permute-done.24 = bf16[64,5120]{1,0:T(8,128)(2,1)S(1)} collective-permute-done((bf16[64,5120]{1,0:T(8,128)(2,1)S(1)}, bf16[64,5120]{1,0:T(8,128)(2,1)S(1)}, u32[]{:S(2)}, u32[]{:S(2)}) %collective-permute-start.24) | collective-permute-done | bytes 655392 | tf_op jit(solution)/shard_map/ppermute | solution.py:48
  311.5 4.8 %collective-permute-start.25 = (bf16[64,5120]{1,0:T(8,128)(2,1)S(1)}, bf16[64,5120]{1,0:T(8,128)(2,1)S(1)}, u32[]{:S(2)}, u32[]{:S(2)}) collective-permute-start(bf16[64,5120]{1,0:T(8,128)(2,1)S(1)} %collective-permute-done.24), channel_id=1, source_target_pairs={{0,1},{1,2},{2,3},{3,0},{4,5},{5,6},{6,7},{7,4},{8,9},{9,10},{10,1... | collective-permute-start | bytes 1966088 | tf_op jit(solution)/shard_map/ppermute | solution.py:48
  318.6 6.7 %collective-permute-start.16 = (bf16[64,5120]{1,0:T(8,128)(2,1)S(1)}, bf16[64,5120]{1,0:T(8,128)(2,1)S(1)}, u32[]{:S(2)}, u32[]{:S(2)}) collective-permute-start(bf16[64,5120]{1,0:T(8,128)(2,1)S(1)} %collective-permute-done.15), channel_id=1, source_target_pairs={{16,17},{17,18},{18,19},{19,16},{20,21},{21,22},{22,23},{23,20},{2... | collective-permute-start | bytes 1966088 | tf_op jit(solution)/shard_map/ppermute | solution.py:47
  325.4 8.0 %collective-permute-done.16 = bf16[64,5120]{1,0:T(8,128)(2,1)S(1)} collective-permute-done((bf16[64,5120]{1,0:T(8,128)(2,1)S(1)}, bf16[64,5120]{1,0:T(8,128)(2,1)S(1)}, u32[]{:S(2)}, u32[]{:S(2)}) %collective-permute-start.16) | collective-permute-done | bytes 655392 | tf_op jit(solution)/shard_map/ppermute | solution.py:47
  (150 shorter events, 83.4 us)
Async XLA Ops:
  9.6 32.0 %collective-permute-start.1 = (bf16[256,2560]{1,0:T(8,128)(2,1)}, bf16[256,2560]{1,0:T(8,128)(2,1)}, u32[]{:S(2)}, u32[]{:S(2)}) collective-permute-start(bf16[256,2560]{1,0:T(8,128)(2,1)} %get-tuple-element.26), channel_id=1, source_target_pairs={{0,8},{4,12},{8,0},{12,4},{1,9},{5,13},{9,1},{13,5},{2,10},{6,14},... | collective-permute-start | bytes 3932168 | tf_op jit(solution)/shard_map/ppermute | solution.py:40
  10.1 58.4 %collective-permute-start.5 = (bf16[256,2560]{1,0:T(8,128)(2,1)}, bf16[256,2560]{1,0:T(8,128)(2,1)}, u32[]{:S(2)}, u32[]{:S(2)}) collective-permute-start(bf16[256,2560]{1,0:T(8,128)(2,1)} %get-tuple-element.25), channel_id=1, source_target_pairs={{16,24},{20,28},{24,16},{28,20},{17,25},{21,29},{25,17},{29,21},{1... | collective-permute-start | bytes 3932168 | tf_op jit(solution)/shard_map/ppermute | solution.py:39
  13.6 56.5 %collective-permute-start.4 = (bf16[1280,640]{1,0:T(8,128)(2,1)S(1)}, bf16[1280,640]{1,0:T(8,128)(2,1)}, u32[]{:S(2)}, u32[]{:S(2)}) collective-permute-start(bf16[1280,640]{1,0:T(8,128)(2,1)S(1)} %bitcast.123), channel_id=1, source_target_pairs={{0,4},{4,0},{8,12},{12,8},{1,5},{5,1},{9,13},{13,9},{2,6},{6,2},{1... | collective-permute-start | bytes 4915208 | tf_op jit(solution)/shard_map/ppermute | solution.py:32
  13.6 60.4 %collective-permute-start = (bf16[1280,640]{1,0:T(8,128)(2,1)}, bf16[1280,640]{1,0:T(8,128)(2,1)}, u32[]{:S(2)}, u32[]{:S(2)}) collective-permute-start(bf16[1280,640]{1,0:T(8,128)(2,1)} %bitcast.3), channel_id=1, source_target_pairs={{0,4},{4,0},{8,12},{12,8},{1,5},{5,1},{9,13},{13,9},{2,6},{6,2},{1... | collective-permute-start | bytes 4915208 | tf_op jit(solution)/shard_map/ppermute | solution.py:32
  107.2 11.8 %collective-permute-start.17 = (bf16[256,640]{1,0:T(8,128)(2,1)S(1)}, bf16[256,640]{1,0:T(8,128)(2,1)S(1)}, u32[]{:S(2)}, u32[]{:S(2)}) collective-permute-start(bf16[256,640]{1,0:T(8,128)(2,1)S(1)} %get-tuple-element.11), channel_id=1, source_target_pairs={{16,0},{17,1},{18,2},{19,3},{20,4},{21,5},{22,6},{23,7},{24,8},{25... | collective-permute-start | bytes 983048 | tf_op jit(solution)/shard_map/ppermute | solution.py:176
  115.2 10.4 %collective-permute-start.9 = (bf16[256,640]{1,0:T(8,128)(2,1)S(1)}, bf16[256,640]{1,0:T(8,128)(2,1)S(1)}, u32[]{:S(2)}, u32[]{:S(2)}) collective-permute-start(bf16[256,640]{1,0:T(8,128)(2,1)S(1)} %broadcast_select_fusion.6), channel_id=1, source_target_pairs={{0,8},{4,12},{8,0},{12,4},{1,9},{5,13},{9,1},{13,5},{2,10},{6,14},... | collective-permute-start | bytes 983048 | tf_op jit(solution)/shard_map/ppermute | solution.py:40
  126.9 69.8 %collective-permute-start.32 = (bf16[1280,640]{1,0:T(8,128)(2,1)S(1)}, bf16[1280,640]{1,0:T(8,128)(2,1)S(1)}, u32[]{:S(2)}, u32[]{:S(2)}) collective-permute-start(bf16[1280,640]{1,0:T(8,128)(2,1)S(1)} %convolution_convert_fusion), channel_id=1, source_target_pairs={{0,4},{4,0},{8,12},{12,8},{1,5},{5,1},{9,13},{13,9},{2,6},{6,2},{1... | collective-permute-start | bytes 4915208 | tf_op jit(solution)/shard_map/ppermute | solution.py:32
  131.5 68.2 %collective-permute-start.31 = (bf16[1280,640]{1,0:T(8,128)(2,1)S(1)}, bf16[1280,640]{1,0:T(8,128)(2,1)S(1)}, u32[]{:S(2)}, u32[]{:S(2)}) collective-permute-start(bf16[1280,640]{1,0:T(8,128)(2,1)S(1)} %convolution_convert_fusion.1), channel_id=1, source_target_pairs={{0,4},{4,0},{8,12},{12,8},{1,5},{5,1},{9,13},{13,9},{2,6},{6,2},{1... | collective-permute-start | bytes 4915208 | tf_op jit(solution)/shard_map/ppermute | solution.py:32
  133.2 21.2 %collective-permute-start.10 = (bf16[2,64,2560]{2,1,0:T(8,128)(2,1)S(1)}, bf16[2,64,2560]{2,1,0:T(8,128)(2,1)S(1)}, u32[]{:S(2)}, u32[]{:S(2)}) collective-permute-start(bf16[2,64,2560]{2,1,0:T(8,128)(2,1)S(1)} %dynamic-slice_bitcast_fusion.1), channel_id=1, source_target_pairs={{16,17},{17,18},{18,19},{19,16},{20,21},{21,22},{22,23},{23,20},{2... | collective-permute-start | bytes 1966088 | tf_op jit(solution)/shard_map/ppermute | solution.py:47
  138.9 29.5 %collective-permute-start.19 = (bf16[2,64,2560]{2,1,0:T(8,128)(2,1)S(1)}, bf16[2,64,2560]{2,1,0:T(8,128)(2,1)S(1)}, u32[]{:S(2)}, u32[]{:S(2)}) collective-permute-start(bf16[2,64,2560]{2,1,0:T(8,128)(2,1)S(1)} %dynamic-slice_bitcast_fusion), channel_id=1, source_target_pairs={{0,1},{1,2},{2,3},{3,0},{4,5},{5,6},{6,7},{7,4},{8,9},{9,10},{10,1... | collective-permute-start | bytes 1966088 | tf_op jit(solution)/shard_map/ppermute | solution.py:48
  154.6 27.9 %collective-permute-start.11 = (bf16[2,64,2560]{2,1,0:T(8,128)(2,1)S(1)}, bf16[2,64,2560]{2,1,0:T(8,128)(2,1)S(1)}, u32[]{:S(2)}, u32[]{:S(2)}) collective-permute-start(bf16[2,64,2560]{2,1,0:T(8,128)(2,1)S(1)} %fusion.33), channel_id=1, source_target_pairs={{16,17},{17,18},{18,19},{19,16},{20,21},{21,22},{22,23},{23,20},{2... | collective-permute-start | bytes 1966088 | tf_op jit(solution)/shard_map/ppermute | solution.py:47
  168.6 27.9 %collective-permute-start.20 = (bf16[2,64,2560]{2,1,0:T(8,128)(2,1)S(1)}, bf16[2,64,2560]{2,1,0:T(8,128)(2,1)S(1)}, u32[]{:S(2)}, u32[]{:S(2)}) collective-permute-start(bf16[2,64,2560]{2,1,0:T(8,128)(2,1)S(1)} %fusion.31), channel_id=1, source_target_pairs={{0,1},{1,2},{2,3},{3,0},{4,5},{5,6},{6,7},{7,4},{8,9},{9,10},{10,1... | collective-permute-start | bytes 1966088 | tf_op jit(solution)/shard_map/ppermute | solution.py:48
  182.7 27.9 %collective-permute-start.12 = (bf16[2,64,2560]{2,1,0:T(8,128)(2,1)S(1)}, bf16[2,64,2560]{2,1,0:T(8,128)(2,1)S(1)}, u32[]{:S(2)}, u32[]{:S(2)}) collective-permute-start(bf16[2,64,2560]{2,1,0:T(8,128)(2,1)S(1)} %fusion.32), channel_id=1, source_target_pairs={{16,17},{17,18},{18,19},{19,16},{20,21},{21,22},{22,23},{23,20},{2... | collective-permute-start | bytes 1966088 | tf_op jit(solution)/shard_map/ppermute | solution.py:47
  196.7 27.6 %collective-permute-start.21 = (bf16[2,64,2560]{2,1,0:T(8,128)(2,1)S(1)}, bf16[2,64,2560]{2,1,0:T(8,128)(2,1)S(1)}, u32[]{:S(2)}, u32[]{:S(2)}) collective-permute-start(bf16[2,64,2560]{2,1,0:T(8,128)(2,1)S(1)} %fusion.30), channel_id=1, source_target_pairs={{0,1},{1,2},{2,3},{3,0},{4,5},{5,6},{6,7},{7,4},{8,9},{9,10},{10,1... | collective-permute-start | bytes 1966088 | tf_op jit(solution)/shard_map/ppermute | solution.py:48
  210.8 14.3 %collective-permute-start.13 = (bf16[64,2560]{1,0:T(8,128)(2,1)S(1)}, bf16[64,2560]{1,0:T(8,128)(2,1)S(1)}, u32[]{:S(2)}, u32[]{:S(2)}) collective-permute-start(bf16[64,2560]{1,0:T(8,128)(2,1)S(1)} %fusion.38), channel_id=1, source_target_pairs={{16,24},{20,28},{24,16},{28,20},{17,25},{21,29},{25,17},{29,21},{1... | collective-permute-start | bytes 983048 | tf_op jit(solution)/shard_map/ppermute | solution.py:39
  240.6 20.3 %collective-permute-start.23 = (bf16[64,5120]{1,0:T(8,128)(2,1)S(1)}, bf16[64,5120]{1,0:T(8,128)(2,1)S(1)}, u32[]{:S(2)}, u32[]{:S(2)}) collective-permute-start(bf16[64,5120]{1,0:T(8,128)(2,1)S(1)} %get-tuple-element.16), channel_id=1, source_target_pairs={{0,1},{1,2},{2,3},{3,0},{4,5},{5,6},{6,7},{7,4},{8,9},{9,10},{10,1... | collective-permute-start | bytes 1966088 | tf_op jit(solution)/shard_map/ppermute | solution.py:48
  240.7 19.5 %collective-permute-start.28 = (f32[1,1280]{1,0:T(1,128)S(1)}, f32[1,1280]{1,0:T(1,128)S(1)}, u32[]{:S(2)}, u32[]{:S(2)}) collective-permute-start(f32[1,1280]{1,0:T(1,128)S(1)} %fusion.44), channel_id=1, source_target_pairs={{0,1},{1,2},{2,3},{3,0},{4,5},{5,6},{6,7},{7,4},{8,9},{9,10},{10,1... | collective-permute-start | bytes 15368 | tf_op jit(solution)/shard_map/ppermute | solution.py:48
  242.0 18.4 %collective-permute-start.29 = (f32[1,1280]{1,0:T(1,128)S(1)}, f32[1,1280]{1,0:T(1,128)S(1)}, u32[]{:S(2)}, u32[]{:S(2)}) collective-permute-start(f32[1,1280]{1,0:T(1,128)S(1)} %fusion.44), channel_id=1, source_target_pairs={{0,2},{1,3},{2,0},{3,1},{4,6},{5,7},{6,4},{7,5},{8,10},{9,11},{10,... | collective-permute-start | bytes 15368 | tf_op jit(solution)/shard_map/ppermute | solution.py:48
  245.1 15.2 %collective-permute-start.30 = (f32[1,1280]{1,0:T(1,128)S(1)}, f32[1,1280]{1,0:T(1,128)S(1)}, u32[]{:S(2)}, u32[]{:S(2)}) collective-permute-start(f32[1,1280]{1,0:T(1,128)S(1)} %fusion.44), channel_id=1, source_target_pairs={{0,3},{1,0},{2,1},{3,2},{4,7},{5,4},{6,5},{7,6},{8,11},{9,8},{10,9... | collective-permute-start | bytes 15368 | tf_op jit(solution)/shard_map/ppermute | solution.py:48
  246.4 57.1 %collective-permute-start.14 = (bf16[64,5120]{1,0:T(8,128)(2,1)S(1)}, bf16[64,5120]{1,0:T(8,128)(2,1)S(1)}, u32[]{:S(2)}, u32[]{:S(2)}) collective-permute-start(bf16[64,5120]{1,0:T(8,128)(2,1)S(1)} %get-tuple-element.18), channel_id=1, source_target_pairs={{16,17},{17,18},{18,19},{19,16},{20,21},{21,22},{22,23},{23,20},{2... | collective-permute-start | bytes 1966088 | tf_op jit(solution)/shard_map/ppermute | solution.py:47
  261.0 50.6 %collective-permute-start.24 = (bf16[64,5120]{1,0:T(8,128)(2,1)S(1)}, bf16[64,5120]{1,0:T(8,128)(2,1)S(1)}, u32[]{:S(2)}, u32[]{:S(2)}) collective-permute-start(bf16[64,5120]{1,0:T(8,128)(2,1)S(1)} %collective-permute-done.23), channel_id=1, source_target_pairs={{0,1},{1,2},{2,3},{3,0},{4,5},{5,6},{6,7},{7,4},{8,9},{9,10},{10,1... | collective-permute-start | bytes 1966088 | tf_op jit(solution)/shard_map/ppermute | solution.py:48
  303.5 15.1 %collective-permute-start.15 = (bf16[64,5120]{1,0:T(8,128)(2,1)S(1)}, bf16[64,5120]{1,0:T(8,128)(2,1)S(1)}, u32[]{:S(2)}, u32[]{:S(2)}) collective-permute-start(bf16[64,5120]{1,0:T(8,128)(2,1)S(1)} %collective-permute-done.14), channel_id=1, source_target_pairs={{16,17},{17,18},{18,19},{19,16},{20,21},{21,22},{22,23},{23,20},{2... | collective-permute-start | bytes 1966088 | tf_op jit(solution)/shard_map/ppermute | solution.py:47
  311.5 24.7 %collective-permute-start.25 = (bf16[64,5120]{1,0:T(8,128)(2,1)S(1)}, bf16[64,5120]{1,0:T(8,128)(2,1)S(1)}, u32[]{:S(2)}, u32[]{:S(2)}) collective-permute-start(bf16[64,5120]{1,0:T(8,128)(2,1)S(1)} %collective-permute-done.24), channel_id=1, source_target_pairs={{0,1},{1,2},{2,3},{3,0},{4,5},{5,6},{6,7},{7,4},{8,9},{9,10},{10,1... | collective-permute-start | bytes 1966088 | tf_op jit(solution)/shard_map/ppermute | solution.py:48
  318.6 14.8 %collective-permute-start.16 = (bf16[64,5120]{1,0:T(8,128)(2,1)S(1)}, bf16[64,5120]{1,0:T(8,128)(2,1)S(1)}, u32[]{:S(2)}, u32[]{:S(2)}) collective-permute-start(bf16[64,5120]{1,0:T(8,128)(2,1)S(1)} %collective-permute-done.15), channel_id=1, source_target_pairs={{16,17},{17,18},{18,19},{19,16},{20,21},{21,22},{22,23},{23,20},{2... | collective-permute-start | bytes 1966088 | tf_op jit(solution)/shard_map/ppermute | solution.py:47
  (32 other events, 237.6 us)

commit v2 on v1

v2 whole, which is shorter than its diff:
```python
import math

import jax
import jax.numpy as jnp
from jax import lax
from jax.experimental import pallas as pl
from jax.experimental.pallas import tpu as pltpu
from jax.sharding import PartitionSpec as P

HEAD = 128
EPS = 1e-06
MASKED = -1e30
CORES = 2
F32 = jnp.float32
BF16 = jnp.bfloat16


def dot_rows(left, right):
    return lax.dot_general(left, right, (((0,), (0,)), ((), ())), preferred_element_type=F32)


def dot_last(left, right):
    return lax.dot_general(left, right, (((1,), (1,)), ((), ())), preferred_element_type=F32)


def dot_plain(left, right):
    return jnp.dot(left, right, preferred_element_type=F32)


BOTH, ENCODER, DECODER = (0, 1), (0,), (1,)


def permute(x, axis, to, sections):
    n = lax.axis_size(axis)
    if sections == BOTH:
        return lax.ppermute(x, axis, [(i, to(i, n)) for i in range(n)])
    pairs = [(s * n + i, s * n + to(i, n)) for s in sections for i in range(n)]
    return lax.ppermute(x, ("section", axis), pairs)


def core_swap(x, sections=BOTH):
    return permute(x, "dp", lambda i, n: i ^ 1, sections)


def chip_shift(x, by, sections=BOTH):
    return permute(x, "dp", lambda i, n: (i + by * CORES) % n, sections)


def home_shift(x, by):
    n = lax.axis_size("dp")
    pairs = [(n + i, (i + by * CORES) % n) for i in range(n)]
    return lax.ppermute(x, ("section", "dp"), pairs)


def head_shift(x, by, sections=BOTH):
    return permute(x, "mp", lambda i, n: (i + by) % n, sections)


def after(x, *before):
    return lax.optimization_barrier((x,) + before)[0]


def attention_kernel(lengths_ref, q_ref, kv_ref, g_ref, ctx_ref, gq_ref, gkv_ref):
    scale = 1.0 / math.sqrt(HEAD)
    q, k, v, g = q_ref[...], kv_ref[0], kv_ref[1], g_ref[...]
    scores = dot_last(q, k) * scale
    column = lax.broadcasted_iota(jnp.int32, scores.shape, 1)
    scores = jnp.where(column < lengths_ref[0, 0], scores, MASKED)
    top = jnp.max(scores, axis=-1, keepdims=True)
    raised = jnp.exp(scores - top)
    weights = raised / jnp.sum(raised, axis=-1, keepdims=True)
    low = weights.astype(BF16)
    ctx_ref[...] = dot_plain(low, v).astype(BF16)
    gkv_ref[1] = dot_rows(low, g).astype(BF16)
    grad_weights = dot_last(g, v)
    centered = grad_weights - jnp.sum(weights * grad_weights, axis=-1, keepdims=True)
    grad_scores = (weights * centered * scale).astype(BF16)
    gq_ref[...] = dot_plain(grad_scores, k).astype(BF16)
    gkv_ref[0] = dot_rows(grad_scores, q).astype(BF16)


def attention(lengths, q, kv, g):
    rows, columns = q.shape
    block = pl.BlockSpec((rows, HEAD), lambda h: (0, h))
    pair = pl.BlockSpec((2, rows, HEAD), lambda h: (0, 0, h))
    shape = jax.ShapeDtypeStruct((rows, columns), BF16)
    heads = columns // HEAD
    return pl.pallas_call(
        attention_kernel,
        grid=(heads,),
        in_specs=[pl.BlockSpec(memory_space=pltpu.SMEM), block, pair, block],
        out_specs=[block, block, pair],
        out_shape=[shape, shape, jax.ShapeDtypeStruct((2, rows, columns), BF16)],
        compiler_params=pltpu.CompilerParams(vmem_limit_bytes=32 * 2**20),
        cost_estimate=pl.CostEstimate(
            flops=14 * rows * rows * columns,
            bytes_accessed=16 * rows * columns,
            transcendentals=heads * rows * rows,
        ),
        name="attention",
    )(lengths, q, kv, g)


def shards(hidden, gain, w_first, w_second, lengths, cotangent):
    encoder = lax.axis_index("section") == 0
    place = lax.axis_index("dp")
    chip, core = place // CORES, lax.rem(place, CORES)
    head_place = lax.axis_index("mp")
    heads_axis = lax.axis_size("mp")
    chips = lax.axis_size("dp") // CORES
    states = hidden[0, 0]
    length, width = states.shape
    gains = gain[0][None, :]
    tile = w_first.shape[1]
    span = CORES * tile
    columns = w_first.shape[2]
    block = length // heads_axis
    others = range(1, chips)

    def chip_at(k):
        return lax.rem(chip + k + chips, chips)

    def chip_columns(array, k):
        return lax.dynamic_slice_in_dim(array, chip_at(k) * span, span, 1)

    def in_order(own, other):
        return jnp.concatenate(
            [jnp.where(core == 0, own, other), jnp.where(core == 0, other, own)], axis=0
        )

    def whole_chip(own):
        return in_order(own, core_swap(own))

    first, second = w_first[0], w_second[0]
    cut = tile // 4
    first_far = [chip_shift(first, k, DECODER) for k in others]
    second_upper = [chip_shift(second[:cut], k, DECODER) for k in others]
    far_states = [chip_shift(chip_columns(states, k), k, ENCODER) for k in others]
    first_chip = whole_chip(first)
    second_chip = whole_chip(second)
    wide = states.astype(F32)
    inverse = lax.rsqrt(jnp.mean(wide * wide, axis=-1, keepdims=True) + EPS)
    inverse_row = inverse.reshape(1, length)
    far_inverse = [chip_shift(inverse_row, k, ENCODER).reshape(length, 1) for k in others]
    unit = wide * inverse
    normed = (unit * gains).astype(BF16)
    keep = jnp.arange(length)[:, None] < lengths[0, 1]
    grad_out = jnp.where(keep, cotangent[0, 0], jnp.zeros((), BF16))

    near_normed = chip_columns(normed, 0)
    second_left = jnp.where(encoder, near_normed, chip_columns(grad_out, 0))
    own_first = dot_plain(near_normed, first_chip)
    own_second = dot_plain(second_left, second_chip)
    normed_columns = [chip_columns(normed, -k) for k in others]
    grad_columns = [chip_columns(grad_out, -k) for k in others]
    far_states, own_first, own_second, normed_columns, grad_columns = lax.optimization_barrier(
        (far_states, own_first, own_second, normed_columns, grad_columns)
    )
    gains_chip = chip_columns(gains, 0)
    far_normed = [
        (rows.astype(F32) * inv * gains_chip).astype(BF16)
        for rows, inv in zip(far_states, far_inverse)
    ]

    both = jnp.stack([own_first, own_second])
    for k in others:
        part = jnp.stack(
            [dot_plain(far_normed[k - 1], w).astype(BF16) for w in (first_chip, second_chip)]
        )
        both = both + chip_shift(part, -k, ENCODER).astype(F32)
    both, first_far, second_upper = lax.optimization_barrier(
        (both.astype(BF16), first_far, second_upper)
    )
    second_lower = [
        chip_shift(after(second[cut:], *second_upper), k, DECODER) for k in others
    ]
    memory_heads = lax.ppermute(both, "section", [(0, 1)])

    first_far = [whole_chip(w) for w in first_far]
    queries, grad_context = own_first, own_second
    for k in others:
        queries = queries + dot_plain(normed_columns[k - 1], first_far[k - 1])
    queries = queries.astype(BF16)
    upper_swapped = [core_swap(w) for w in second_upper]
    memory_heads, second_lower, queries, upper_swapped = lax.optimization_barrier(
        (memory_heads, second_lower, queries, upper_swapped)
    )
    second_far = [
        in_order(
            jnp.concatenate([second_upper[i], second_lower[i]], axis=0),
            jnp.concatenate([upper_swapped[i], core_swap(second_lower[i])], axis=0),
        )
        for i in range(chips - 1)
    ]
    for k in others:
        grad_context = grad_context + dot_plain(grad_columns[k - 1], second_far[k - 1])
    context, grad_query, grad_memory = attention(
        lengths, queries, memory_heads, grad_context.astype(BF16)
    )
    grad_memory, *far_memory = [home_shift(grad_memory, k) for k in range(chips)]

    def block_at(array, place):
        at = lax.rem(place + 2 * heads_axis, heads_axis) * block
        return lax.dynamic_slice_in_dim(array, at, block, array.ndim - 2)

    def first_block(parts):
        return block_at(parts, head_place - 1)

    def summed(got, parts, step):
        return got.astype(F32) + block_at(parts, head_place - 2 - step).astype(F32)

    def my_rows(array):
        return block_at(array, head_place)

    def place_rows(whole, rows, step, column=0):
        at = lax.rem(head_place - step + heads_axis, heads_axis) * block
        return lax.dynamic_update_slice(whole, rows, (at, column))

    def piled(parts):
        return jnp.stack([p.astype(BF16) for p in parts])

    last = heads_axis - 1
    out_parts = piled(dot_last(context, w) for w in [second_chip] + second_far)
    grad_query_later = after(grad_query, out_parts)
    back_parts = piled(dot_last(grad_query_later, w) for w in [first_chip] + first_far)

    def send_out(x):
        return head_shift(x, 1, DECODER)

    def send_memory(x):
        return head_shift(x, 1, ENCODER)

    out_held, back_held = first_block(out_parts), first_block(back_parts)
    out_got, back_got = send_out(out_held), send_out(back_held)
    for step in range(last):
        out_sum = summed(after(out_got, back_held), out_parts, step)
        out_held = out_sum.astype(BF16)
        if step < last - 1:
            out_got = send_out(out_held)
        back_sum = summed(after(back_got, out_held), back_parts, step)
        back_held = back_sum.astype(BF16)
        if step < last - 1:
            back_got = send_out(back_held)
        if step == 0:
            round_done = out_held
            memory_parts = piled(
                dot_last(g[0], first_chip) + dot_last(g[1], second_chip)
                for g in [after(grad_memory, back_held)] + far_memory
            )
            memory_held = first_block(memory_parts)
            memory_got = send_memory(memory_held)
        else:
            memory_sum = summed(after(memory_got, back_held), memory_parts, step - 1)
            memory_held = memory_sum.astype(BF16)
            memory_got = send_memory(memory_held)
    memory_sum = summed(memory_got, memory_parts, last - 1)

    def whole_rows(pieces):
        whole = jnp.zeros((block, width), F32)
        for k in range(chips):
            whole = lax.dynamic_update_slice_in_dim(whole, pieces[k], chip_at(-k) * span, 1)
        return whole

    out_rows = (my_rows(states).astype(F32) + whole_rows(out_sum)).astype(BF16)
    homes = [chip_shift(memory_sum[k].astype(BF16), -k, ENCODER).astype(F32) for k in others]
    grad_normed = whole_rows(
        [jnp.where(encoder, memory_sum[0], back_sum[0])]
        + [jnp.where(encoder, homes[chips - 1 - k], back_sum[k]) for k in others]
    )
    grad_normed = grad_normed + jnp.where(encoder, my_rows(cotangent[0, 0]).astype(F32), 0.0)
    my_inverse = my_rows(inverse)
    my_unit = my_rows(states).astype(F32) * my_inverse
    residual = jnp.where(encoder, 0.0, my_rows(grad_out).astype(F32))
    scaled = grad_normed * gains
    inner = jnp.mean(scaled * my_unit, axis=-1, keepdims=True)
    grad_rows = (my_inverse * (scaled - my_unit * inner) + residual).astype(BF16)

    output = place_rows(jnp.zeros((length, width), BF16), out_rows, 0)
    grad_states = place_rows(jnp.zeros((length, width), BF16), grad_rows, 0)
    out_held, back_held = out_rows, grad_rows
    out_got = head_shift(out_held, 1, DECODER)
    back_got = head_shift(back_held, 1)
    for step in range(1, last + 1):
        out_held = after(out_got, back_held)
        output = place_rows(output, out_held, step)
        if step < last:
            out_got = head_shift(out_held, 1, DECODER)
        back_held = after(back_got, out_held)
        grad_states = place_rows(grad_states, back_held, step)
        if step == 1:
            first_arrival = back_held
        if step < last:
            back_got = head_shift(back_held, 1)
    result = jnp.where(encoder, normed, output)

    gain_part = jnp.sum(grad_normed * my_unit, axis=0, keepdims=True)
    gain_parts = [head_shift(gain_part, k) for k in range(1, heads_axis)]
    gain_parts = after(gain_parts, first_arrival)
    for part in gain_parts:
        gain_part = gain_part + part
    gain_chip = chip_columns(gain_part, 0)
    for k in others:
        gain_chip = gain_chip + chip_shift(chip_columns(gain_part, k), k)
    gain_sum = lax.dynamic_slice_in_dim(gain_chip, core * tile, tile, 1)
    gain_sum = gain_sum + core_swap(
        lax.dynamic_slice_in_dim(gain_chip, (1 - core) * tile, tile, 1)
    )

    left, right = [near_normed], [second_left]
    grads_first = [jnp.where(encoder, grad_memory[0], grad_query)]
    grads_second = [jnp.where(encoder, grad_memory[1], context)]
    for k in others:
        moved = chip_shift(after(chip_columns(normed, k), round_done), k, DECODER)
        left.append(jnp.where(encoder, far_normed[k - 1], moved))
        moved = chip_shift(after(chip_columns(grad_out, k), round_done), k, DECODER)
        right.append(jnp.where(encoder, far_normed[k - 1], moved))
        moved = chip_shift(after(grad_query, round_done), k, DECODER)
        grads_first.append(jnp.where(encoder, far_memory[k - 1][0], moved))
        moved = chip_shift(after(context, round_done), k, DECODER)
        grads_second.append(jnp.where(encoder, far_memory[k - 1][1], moved))

    def weight_grad(rows, grads):
        rows, grads = jnp.concatenate(rows, axis=0), jnp.concatenate(grads, axis=0)
        own = dot_rows(lax.dynamic_slice_in_dim(rows, core * tile, tile, 1), grads)
        other = dot_rows(lax.dynamic_slice_in_dim(rows, (1 - core) * tile, tile, 1), grads)
        return own + core_swap(other.astype(BF16)).astype(F32)

    first_sum = weight_grad(left, grads_first)
    second_sum = weight_grad(right, grads_second)
    return (
        result[None, None],
        grad_states[None, None],
        gain_sum,
        first_sum[None],
        second_sum[None],
    )


def solution(mesh):
    return jax.shard_map(
        shards,
        mesh=mesh,
        in_specs=(
            P("section", "dp", None, None),
            P("section", None),
            P("section", "dp", "mp"),
            P("section", "dp", "mp"),
            P("dp", None),
            P("section", "dp", None, None),
        ),
        out_specs=(
            P("section", "dp", None, None),
            P("section", "dp", None, None),
            P("section", "dp"),
            P("section", "dp", "mp"),
            P("section", "dp", "mp"),
        ),
        check_vma=False,
    )
```

time: 342 us -> 310 us (0.906)
  waiting for transfers between devices: 191 us -> 165 us
  starting transfers between devices: 90 us -> 64.2 us
  local copies, waits for them, and re-layouts: 4.93 us -> 19.2 us
  matrix products: 24.1 us -> 28.1 us
  other arithmetic: 21.3 us -> 24.8 us
    ppermute x33 -> x41, starting transfers between devices: 90 us -> 64.2 us  [the longest x23 49.8 us: permute(): return lax.ppermute(x, ('section', axis), pairs)]
    ppermute x33 -> x41, waiting for transfers between devices: 191 us -> 165 us  [the longest x23 114 us: permute(): return lax.ppermute(x, ('section', axis), pairs)]
    unnamed x46 -> x58, local copies, waits for them, and re-layouts: 2.85 us -> 11.7 us
    dot_general x4 -> x8, matrix products: 6.47 us -> 9.79 us  [dot_last(): lax.dot_general(left, right, (((1,), (1,)), ((), ())), preferred_element_...]
    dot_general x4 -> x6, matrix products: 7.15 us -> 9.95 us  [dot_plain(): return jnp.dot(left, right, preferred_element_type=F32)]
  transfers between devices with their start and end apart: 33 -> 41, of which waited for: 23 -> 15; matrix products, arithmetic and copies ran while one was open for 12% -> 18% of each run, Pallas kernels for 0% -> 0%
where the time goes in v2:
time: 310 us; the launch traced here: 308 us
  waiting for transfers between devices  165 us (53%)
  starting transfers between devices  64.2 us (21%)
  matrix products  28.1 us (9%)
  other arithmetic  24.8 us (8%)
  local copies, waits for them, and re-layouts  19.2 us (6%)
  Pallas kernels  4.9 us (2%)
    ppermute x23, waiting for transfers between devices, permute(): return lax.ppermute(x, ('section', axis), pairs)  114 us
    ppermute x23, starting transfers between devices, permute(): return lax.ppermute(x, ('section', axis), pairs)  49.8 us
    ppermute x15, waiting for transfers between devices, permute(): return lax.ppermute(x, axis, [(i, to(i, n)) for i in range(n)])  27.6 us
    ppermute x1, waiting for transfers between devices, shards(): memory_heads = lax.ppermute(both, 'section', [(0, 1)])  23.3 us
    unnamed x58, local copies, waits for them, and re-layouts  11.7 us
    ppermute x15, starting transfers between devices, permute(): return lax.ppermute(x, axis, [(i, to(i, n)) for i in range(n)])  10.3 us
    dot_general x6, matrix products, dot_plain(): return jnp.dot(left, right, preferred_element_type=F32)  9.95 us
    dot_general x8, matrix products, dot_last(): lax.dot_general(left, right, (((1,), (1,)), ((), ())), preferred_element_...  9.79 us
  transfers between devices with their start and end apart: 41, of which 15 were waited for; matrix products, arithmetic and copies ran while one was open for 18% of the time, Pallas kernels for 0%

profile of v2, /device:TPU:6, one launch (start us, length us, event | category | flops | bytes accessed | tf_op | source)
XLA Modules:
  0.0 308.2 jit_solution(13970929503172970231)
XLA Ops:
  32.3 3.4 %collective-permute-start.6 = (bf16[320,640]{1,0:T(8,128)(2,1)S(1)}, bf16[320,640]{1,0:T(8,128)(2,1)S(1)}, u32[]{:S(2)}, u32[]{:S(2)}) collective-permute-start(bf16[320,640]{1,0:T(8,128)(2,1)S(1)} %slice_bitcast_fusion.4), channel_id=1, source_target_pairs={{16,24},{20,28},{24,16},{28,20},{17,25},{21,29},{25,17},{29,21},{1... | collective-permute-start | bytes 1228808 | tf_op jit(solution)/shard_map/ppermute | solution.py:38
  35.9 14.0 %collective-permute-done.6 = bf16[320,640]{1,0:T(8,128)(2,1)S(1)} collective-permute-done((bf16[320,640]{1,0:T(8,128)(2,1)S(1)}, bf16[320,640]{1,0:T(8,128)(2,1)S(1)}, u32[]{:S(2)}, u32[]{:S(2)}) %collective-permute-start.6) | collective-permute-done | bytes 409632 | tf_op jit(solution)/shard_map/ppermute | solution.py:38
  57.7 23.3 %collective-permute-done.7.kv_ref = bf16[2,256,640]{2,1,0:T(8,128)(2,1)S(1)} collective-permute-done((bf16[2,256,640]{2,1,0:T(8,128)(2,1)S(1)}, bf16[2,256,640]{2,1,0:T(8,128)(2,1)S(1)}, u32[]{:S(2)}, u32[]{:S(2)}) %collective-permute-start.7) | collective-permute-done | bytes 655392 | tf_op jit(solution)/shard_map/ppermute | solution.py:177
  89.2 4.9 %attention.1 = (bf16[256,640]{1,0:T(8,128)(2,1)S(1)}, bf16[256,640]{1,0:T(8,128)(2,1)S(1)}, bf16[2,256,640]{2,1,0:T(8,128)(2,1)S(1)}) custom-call(s32[1,2]{1,0:T(1,128)S(1)} %copy-done, bf16[256,640]{1,0:T(8,128)(2,1)S(1)} %fusion.37.q_ref, bf16[2,256,640]{2,1,0:T(8,128)(2,1)S(1)} %collective-permute-done.7.kv_ref, bf16[256,640]{1,0:T(8,128)(2,1)S(1)} %fusion.36.g_ref), custom_call_target="tpu_custom_call" | custom-call | flops 587202560 | bytes 2621440 | tf_op jit(solution)/shard_map/attention/pallas_call | solution.py:88
  100.8 3.7 %collective-permute-start.12 = (bf16[2,64,2560]{2,1,0:T(8,128)(2,1)S(1)}, bf16[2,64,2560]{2,1,0:T(8,128)(2,1)S(1)}, u32[]{:S(2)}, u32[]{:S(2)}) collective-permute-start(bf16[2,64,2560]{2,1,0:T(8,128)(2,1)S(1)} %fusion.48), channel_id=1, source_target_pairs={{16,17},{17,18},{18,19},{19,16},{20,21},{21,22},{22,23},{23,20},{2... | collective-permute-start | bytes 1966088 | tf_op jit(solution)/shard_map/ppermute | solution.py:38
  105.8 3.5 %collective-permute-start.14 = (bf16[2,64,2560]{2,1,0:T(8,128)(2,1)S(1)}, bf16[2,64,2560]{2,1,0:T(8,128)(2,1)S(1)}, u32[]{:S(2)}, u32[]{:S(2)}) collective-permute-start(bf16[2,64,2560]{2,1,0:T(8,128)(2,1)S(1)} %fusion.45), channel_id=1, source_target_pairs={{16,17},{17,18},{18,19},{19,16},{20,21},{21,22},{22,23},{23,20},{2... | collective-permute-start | bytes 1966088 | tf_op jit(solution)/shard_map/ppermute | solution.py:38
  109.3 12.9 %collective-permute-done.12 = bf16[2,64,2560]{2,1,0:T(8,128)(2,1)S(1)} collective-permute-done((bf16[2,64,2560]{2,1,0:T(8,128)(2,1)S(1)}, bf16[2,64,2560]{2,1,0:T(8,128)(2,1)S(1)}, u32[]{:S(2)}, u32[]{:S(2)}) %collective-permute-start.12) | collective-permute-done | bytes 655392 | tf_op jit(solution)/shard_map/ppermute | solution.py:38
  124.3 3.1 %collective-permute-start.36 = (bf16[256,640]{1,0:T(8,128)(2,1)S(1)}, bf16[256,640]{1,0:T(8,128)(2,1)S(1)}, u32[]{:S(2)}, u32[]{:S(2)}) collective-permute-start(bf16[256,640]{1,0:T(8,128)(2,1)S(1)} %get-tuple-element.76), channel_id=1, source_target_pairs={{16,24},{20,28},{24,16},{28,20},{17,25},{21,29},{25,17},{29,21},{1... | collective-permute-start | bytes 983048 | tf_op jit(solution)/shard_map/ppermute | solution.py:38
  127.4 8.8 %collective-permute-done.14 = bf16[2,64,2560]{2,1,0:T(8,128)(2,1)S(1)} collective-permute-done((bf16[2,64,2560]{2,1,0:T(8,128)(2,1)S(1)}, bf16[2,64,2560]{2,1,0:T(8,128)(2,1)S(1)}, u32[]{:S(2)}, u32[]{:S(2)}) %collective-permute-start.14) | collective-permute-done | bytes 655392 | tf_op jit(solution)/shard_map/ppermute | solution.py:38
  136.3 3.1 %collective-permute-start.39 = (bf16[256,640]{1,0:T(8,128)(2,1)S(1)}, bf16[256,640]{1,0:T(8,128)(2,1)S(1)}, u32[]{:S(2)}, u32[]{:S(2)}) collective-permute-start(bf16[256,640]{1,0:T(8,128)(2,1)S(1)} %get-tuple-element.78), channel_id=1, source_target_pairs={{16,24},{20,28},{24,16},{28,20},{17,25},{21,29},{25,17},{29,21},{1... | collective-permute-start | bytes 983048 | tf_op jit(solution)/shard_map/ppermute | solution.py:38
  150.9 3.1 %collective-permute-start.38 = (bf16[256,2560]{1,0:T(8,128)(2,1)S(1)}, bf16[256,2560]{1,0:T(8,128)(2,1)S(1)}, u32[]{:S(2)}, u32[]{:S(2)}) collective-permute-start(bf16[256,2560]{1,0:T(8,128)(2,1)S(1)} %copy-done.23), channel_id=1, source_target_pairs={{16,24},{20,28},{24,16},{28,20},{17,25},{21,29},{25,17},{29,21},{1... | collective-permute-start | bytes 3932168 | tf_op jit(solution)/shard_map/ppermute | solution.py:38
  155.0 3.3 %collective-permute-start.15 = (bf16[2,64,2560]{2,1,0:T(8,128)(2,1)S(1)}, bf16[2,64,2560]{2,1,0:T(8,128)(2,1)S(1)}, u32[]{:S(2)}, u32[]{:S(2)}) collective-permute-start(bf16[2,64,2560]{2,1,0:T(8,128)(2,1)S(1)} %add_convert_fusion.3), channel_id=1, source_target_pairs={{16,17},{17,18},{18,19},{19,16},{20,21},{21,22},{22,23},{23,20},{2... | collective-permute-start | bytes 1966088 | tf_op jit(solution)/shard_map/ppermute | solution.py:38
  158.2 6.1 %collective-permute-done.16 = bf16[2,64,2560]{2,1,0:T(8,128)(2,1)S(1)} collective-permute-done((bf16[2,64,2560]{2,1,0:T(8,128)(2,1)S(1)}, bf16[2,64,2560]{2,1,0:T(8,128)(2,1)S(1)}, u32[]{:S(2)}, u32[]{:S(2)}) %collective-permute-start.16) | collective-permute-done | bytes 655392 | tf_op jit(solution)/shard_map/ppermute | solution.py:38
  167.5 10.2 %collective-permute-done.35 = bf16[256,2560]{1,0:T(8,128)(2,1)S(1)} collective-permute-done((bf16[256,2560]{1,0:T(8,128)(2,1)S(1)}, bf16[256,2560]{1,0:T(8,128)(2,1)S(1)}, u32[]{:S(2)}, u32[]{:S(2)}) %collective-permute-start.35) | collective-permute-done | bytes 1310752 | tf_op jit(solution)/shard_map/ppermute | solution.py:38
  177.6 25.8 %collective-permute-done.38 = bf16[256,2560]{1,0:T(8,128)(2,1)S(1)} collective-permute-done((bf16[256,2560]{1,0:T(8,128)(2,1)S(1)}, bf16[256,2560]{1,0:T(8,128)(2,1)S(1)}, u32[]{:S(2)}, u32[]{:S(2)}) %collective-permute-start.38) | collective-permute-done | bytes 1310752 | tf_op jit(solution)/shard_map/ppermute | solution.py:38
  223.9 9.0 %collective-permute-done.17 = bf16[64,5120]{1,0:T(8,128)(2,1)S(1)} collective-permute-done((bf16[64,5120]{1,0:T(8,128)(2,1)S(1)}, bf16[64,5120]{1,0:T(8,128)(2,1)S(1)}, u32[]{:S(2)}, u32[]{:S(2)}) %collective-permute-start.17) | collective-permute-done | bytes 655392 | tf_op jit(solution)/shard_map/ppermute | solution.py:38
  232.9 3.9 %collective-permute-start.32 = (f32[1,5120]{1,0:T(1,128)S(1)}, f32[1,5120]{1,0:T(1,128)S(1)}, u32[]{:S(2)}, u32[]{:S(2)}) collective-permute-start(f32[1,5120]{1,0:T(1,128)S(1)} %bitcast.137), channel_id=1, source_target_pairs={{0,3},{1,0},{2,1},{3,2},{4,7},{5,4},{6,5},{7,6},{8,11},{9,8},{10,9... | collective-permute-start | bytes 61448 | tf_op jit(solution)/shard_map/ppermute | solution.py:36
  236.8 3.0 fusion.12
  241.9 3.0 fusion.11
  244.9 7.5 %collective-permute-done.26 = bf16[64,5120]{1,0:T(8,128)(2,1)S(1)} collective-permute-done((bf16[64,5120]{1,0:T(8,128)(2,1)S(1)}, bf16[64,5120]{1,0:T(8,128)(2,1)S(1)}, u32[]{:S(2)}, u32[]{:S(2)}) %collective-permute-start.26) | collective-permute-done | bytes 655392 | tf_op jit(solution)/shard_map/ppermute | solution.py:36
  253.8 13.0 %collective-permute-done.25 = bf16[64,5120]{1,0:T(8,128)(2,1)S(1)} collective-permute-done((bf16[64,5120]{1,0:T(8,128)(2,1)S(1)}, bf16[64,5120]{1,0:T(8,128)(2,1)S(1)}, u32[]{:S(2)}, u32[]{:S(2)}) %collective-permute-start.25) | collective-permute-done | bytes 655392 | tf_op jit(solution)/shard_map/ppermute | solution.py:38
  270.7 10.2 %collective-permute-done.28 = bf16[64,5120]{1,0:T(8,128)(2,1)S(1)} collective-permute-done((bf16[64,5120]{1,0:T(8,128)(2,1)S(1)}, bf16[64,5120]{1,0:T(8,128)(2,1)S(1)}, u32[]{:S(2)}, u32[]{:S(2)}) %collective-permute-start.28) | collective-permute-done | bytes 655392 | tf_op jit(solution)/shard_map/ppermute | solution.py:36
  280.9 14.0 %collective-permute-done.27 = bf16[64,5120]{1,0:T(8,128)(2,1)S(1)} collective-permute-done((bf16[64,5120]{1,0:T(8,128)(2,1)S(1)}, bf16[64,5120]{1,0:T(8,128)(2,1)S(1)}, u32[]{:S(2)}, u32[]{:S(2)}) %collective-permute-start.27) | collective-permute-done | bytes 655392 | tf_op jit(solution)/shard_map/ppermute | solution.py:38
  297.8 8.8 %collective-permute-done.29 = bf16[64,5120]{1,0:T(8,128)(2,1)S(1)} collective-permute-done((bf16[64,5120]{1,0:T(8,128)(2,1)S(1)}, bf16[64,5120]{1,0:T(8,128)(2,1)S(1)}, u32[]{:S(2)}, u32[]{:S(2)}) %collective-permute-start.29) | collective-permute-done | bytes 655392 | tf_op jit(solution)/shard_map/ppermute | solution.py:36
  (195 shorter events, 104.8 us)
Async XLA Ops:
  0.6 21.4 %collective-permute-start.1 = (bf16[1280,640]{1,0:T(8,128)(2,1)}, bf16[1280,640]{1,0:T(8,128)(2,1)}, u32[]{:S(2)}, u32[]{:S(2)}) collective-permute-start(bf16[1280,640]{1,0:T(8,128)(2,1)} %bitcast.127), channel_id=1, source_target_pairs={{0,4},{4,0},{8,12},{12,8},{1,5},{5,1},{9,13},{13,9},{2,6},{6,2},{1... | collective-permute-start | bytes 4915208 | tf_op jit(solution)/shard_map/ppermute | solution.py:36
  0.7 49.2 %collective-permute-start.5 = (bf16[1280,640]{1,0:T(8,128)(2,1)}, bf16[1280,640]{1,0:T(8,128)(2,1)}, u32[]{:S(2)}, u32[]{:S(2)}) collective-permute-start(bf16[1280,640]{1,0:T(8,128)(2,1)} %bitcast.128), channel_id=1, source_target_pairs={{16,24},{20,28},{24,16},{28,20},{17,25},{21,29},{25,17},{29,21},{1... | collective-permute-start | bytes 4915208 | tf_op jit(solution)/shard_map/ppermute | solution.py:38
  50.1 31.4 %collective-permute-start.8 = (bf16[960,640]{1,0:T(8,128)(2,1)S(1)}, bf16[960,640]{1,0:T(8,128)(2,1)}, u32[]{:S(2)}, u32[]{:S(2)}) collective-permute-start(bf16[960,640]{1,0:T(8,128)(2,1)S(1)} %slice_bitcast_fusion), channel_id=1, source_target_pairs={{16,24},{20,28},{24,16},{28,20},{17,25},{21,29},{25,17},{29,21},{1... | collective-permute-start | bytes 3686408 | tf_op jit(solution)/shard_map/ppermute | solution.py:38
  52.8 28.3 %collective-permute-start.7 = (bf16[2,256,640]{2,1,0:T(8,128)(2,1)S(1)}, bf16[2,256,640]{2,1,0:T(8,128)(2,1)S(1)}, u32[]{:S(2)}, u32[]{:S(2)}) collective-permute-start(bf16[2,256,640]{2,1,0:T(8,128)(2,1)S(1)} %fusion.33), channel_id=1, source_target_pairs={{0,16},{1,17},{2,18},{3,19},{4,20},{5,21},{6,22},{7,23},{8,24},{9,... | collective-permute-start | bytes 1966088 | tf_op jit(solution)/shard_map/ppermute | solution.py:177
  96.8 42.8 %collective-permute-start.18 = (bf16[2,256,640]{2,1,0:T(8,128)(2,1)S(1)}, bf16[2,256,640]{2,1,0:T(8,128)(2,1)S(1)}, u32[]{:S(2)}, u32[]{:S(2)}) collective-permute-start(bf16[2,256,640]{2,1,0:T(8,128)(2,1)S(1)} %get-tuple-element.63), channel_id=1, source_target_pairs={{16,0},{20,4},{24,8},{28,12},{17,1},{21,5},{25,9},{29,13},{18,2},{... | collective-permute-start | bytes 1966088 | tf_op jit(solution)/shard_map/ppermute | solution.py:52
  98.1 45.9 %collective-permute-start.19 = (bf16[2,256,640]{2,1,0:T(8,128)(2,1)S(1)}, bf16[2,256,640]{2,1,0:T(8,128)(2,1)S(1)}, u32[]{:S(2)}, u32[]{:S(2)}) collective-permute-start(bf16[2,256,640]{2,1,0:T(8,128)(2,1)S(1)} %get-tuple-element.63), channel_id=1, source_target_pairs={{16,8},{20,12},{24,0},{28,4},{17,9},{21,13},{25,1},{29,5},{18,10},... | collective-permute-start | bytes 1966088 | tf_op jit(solution)/shard_map/ppermute | solution.py:52
  100.8 21.5 %collective-permute-start.12 = (bf16[2,64,2560]{2,1,0:T(8,128)(2,1)S(1)}, bf16[2,64,2560]{2,1,0:T(8,128)(2,1)S(1)}, u32[]{:S(2)}, u32[]{:S(2)}) collective-permute-start(bf16[2,64,2560]{2,1,0:T(8,128)(2,1)S(1)} %fusion.48), channel_id=1, source_target_pairs={{16,17},{17,18},{18,19},{19,16},{20,21},{21,22},{22,23},{23,20},{2... | collective-permute-start | bytes 1966088 | tf_op jit(solution)/shard_map/ppermute | solution.py:38
  105.8 30.4 %collective-permute-start.14 = (bf16[2,64,2560]{2,1,0:T(8,128)(2,1)S(1)}, bf16[2,64,2560]{2,1,0:T(8,128)(2,1)S(1)}, u32[]{:S(2)}, u32[]{:S(2)}) collective-permute-start(bf16[2,64,2560]{2,1,0:T(8,128)(2,1)S(1)} %fusion.45), channel_id=1, source_target_pairs={{16,17},{17,18},{18,19},{19,16},{20,21},{21,22},{22,23},{23,20},{2... | collective-permute-start | bytes 1966088 | tf_op jit(solution)/shard_map/ppermute | solution.py:38
  122.4 32.4 %collective-permute-start.13 = (bf16[2,64,2560]{2,1,0:T(8,128)(2,1)S(1)}, bf16[2,64,2560]{2,1,0:T(8,128)(2,1)S(1)}, u32[]{:S(2)}, u32[]{:S(2)}) collective-permute-start(bf16[2,64,2560]{2,1,0:T(8,128)(2,1)S(1)} %add_convert_fusion.5), channel_id=1, source_target_pairs={{16,17},{17,18},{18,19},{19,16},{20,21},{21,22},{22,23},{23,20},{2... | collective-permute-start | bytes 1966088 | tf_op jit(solution)/shard_map/ppermute | solution.py:38
  124.3 25.3 %collective-permute-start.36 = (bf16[256,640]{1,0:T(8,128)(2,1)S(1)}, bf16[256,640]{1,0:T(8,128)(2,1)S(1)}, u32[]{:S(2)}, u32[]{:S(2)}) collective-permute-start(bf16[256,640]{1,0:T(8,128)(2,1)S(1)} %get-tuple-element.76), channel_id=1, source_target_pairs={{16,24},{20,28},{24,16},{28,20},{17,25},{21,29},{25,17},{29,21},{1... | collective-permute-start | bytes 983048 | tf_op jit(solution)/shard_map/ppermute | solution.py:38
  139.6 24.8 %collective-permute-start.16 = (bf16[2,64,2560]{2,1,0:T(8,128)(2,1)S(1)}, bf16[2,64,2560]{2,1,0:T(8,128)(2,1)S(1)}, u32[]{:S(2)}, u32[]{:S(2)}) collective-permute-start(bf16[2,64,2560]{2,1,0:T(8,128)(2,1)S(1)} %add_convert_fusion.4), channel_id=1, source_target_pairs={{16,17},{17,18},{18,19},{19,16},{20,21},{21,22},{22,23},{23,20},{2... | collective-permute-start | bytes 1966088 | tf_op jit(solution)/shard_map/ppermute | solution.py:38
  144.0 33.6 %collective-permute-start.35 = (bf16[256,2560]{1,0:T(8,128)(2,1)S(1)}, bf16[256,2560]{1,0:T(8,128)(2,1)S(1)}, u32[]{:S(2)}, u32[]{:S(2)}) collective-permute-start(bf16[256,2560]{1,0:T(8,128)(2,1)S(1)} %copy-done.24), channel_id=1, source_target_pairs={{16,24},{20,28},{24,16},{28,20},{17,25},{21,29},{25,17},{29,21},{1... | collective-permute-start | bytes 3932168 | tf_op jit(solution)/shard_map/ppermute | solution.py:38
  150.9 52.6 %collective-permute-start.38 = (bf16[256,2560]{1,0:T(8,128)(2,1)S(1)}, bf16[256,2560]{1,0:T(8,128)(2,1)S(1)}, u32[]{:S(2)}, u32[]{:S(2)}) collective-permute-start(bf16[256,2560]{1,0:T(8,128)(2,1)S(1)} %copy-done.23), channel_id=1, source_target_pairs={{16,24},{20,28},{24,16},{28,20},{17,25},{21,29},{25,17},{29,21},{1... | collective-permute-start | bytes 3932168 | tf_op jit(solution)/shard_map/ppermute | solution.py:38
  155.0 54.7 %collective-permute-start.15 = (bf16[2,64,2560]{2,1,0:T(8,128)(2,1)S(1)}, bf16[2,64,2560]{2,1,0:T(8,128)(2,1)S(1)}, u32[]{:S(2)}, u32[]{:S(2)}) collective-permute-start(bf16[2,64,2560]{2,1,0:T(8,128)(2,1)S(1)} %add_convert_fusion.3), channel_id=1, source_target_pairs={{16,17},{17,18},{18,19},{19,16},{20,21},{21,22},{22,23},{23,20},{2... | collective-permute-start | bytes 1966088 | tf_op jit(solution)/shard_map/ppermute | solution.py:38
  164.5 50.1 %collective-permute-start.23 = (bf16[2,64,2560]{2,1,0:T(8,128)(2,1)S(1)}, bf16[2,64,2560]{2,1,0:T(8,128)(2,1)S(1)}, u32[]{:S(2)}, u32[]{:S(2)}) collective-permute-start(bf16[2,64,2560]{2,1,0:T(8,128)(2,1)S(1)} %add_convert_fusion.2), channel_id=1, source_target_pairs={{16,17},{17,18},{18,19},{19,16},{20,21},{21,22},{22,23},{23,20},{2... | collective-permute-start | bytes 1966088 | tf_op jit(solution)/shard_map/ppermute | solution.py:38
  166.6 42.1 %collective-permute-start.21 = (bf16[2,64,2560]{2,1,0:T(8,128)(2,1)S(1)}, bf16[2,64,2560]{2,1,0:T(8,128)(2,1)S(1)}, u32[]{:S(2)}, u32[]{:S(2)}) collective-permute-start(bf16[2,64,2560]{2,1,0:T(8,128)(2,1)S(1)} %add_convert_fusion.1), channel_id=1, source_target_pairs={{0,1},{1,2},{2,3},{3,0},{4,5},{5,6},{6,7},{7,4},{8,9},{9,10},{10,1... | collective-permute-start | bytes 1966088 | tf_op jit(solution)/shard_map/ppermute | solution.py:38
  206.9 26.1 %collective-permute-start.40 = (bf16[1280,640]{1,0:T(8,128)(2,1)S(1)}, bf16[1280,640]{1,0:T(8,128)(2,1)S(1)}, u32[]{:S(2)}, u32[]{:S(2)}) collective-permute-start(bf16[1280,640]{1,0:T(8,128)(2,1)S(1)} %convolution_convert_fusion.4), channel_id=1, source_target_pairs={{0,4},{4,0},{8,12},{12,8},{1,5},{5,1},{9,13},{13,9},{2,6},{6,2},{1... | collective-permute-start | bytes 4915208 | tf_op jit(solution)/shard_map/ppermute | solution.py:36
  208.2 31.6 %collective-permute-start.37 = (bf16[1280,640]{1,0:T(8,128)(2,1)S(1)}, bf16[1280,640]{1,0:T(8,128)(2,1)S(1)}, u32[]{:S(2)}, u32[]{:S(2)}) collective-permute-start(bf16[1280,640]{1,0:T(8,128)(2,1)S(1)} %convolution_convert_fusion.5), channel_id=1, source_target_pairs={{0,4},{4,0},{8,12},{12,8},{1,5},{5,1},{9,13},{13,9},{2,6},{6,2},{1... | collective-permute-start | bytes 4915208 | tf_op jit(solution)/shard_map/ppermute | solution.py:36
  218.2 34.2 %collective-permute-start.30 = (f32[1,5120]{1,0:T(1,128)S(1)}, f32[1,5120]{1,0:T(1,128)S(1)}, u32[]{:S(2)}, u32[]{:S(2)}) collective-permute-start(f32[1,5120]{1,0:T(1,128)S(1)} %bitcast.135), channel_id=1, source_target_pairs={{0,1},{1,2},{2,3},{3,0},{4,5},{5,6},{6,7},{7,4},{8,9},{9,10},{10,1... | collective-permute-start | bytes 61448 | tf_op jit(solution)/shard_map/ppermute | solution.py:36
  219.8 32.6 %collective-permute-start.31 = (f32[1,5120]{1,0:T(1,128)S(1)}, f32[1,5120]{1,0:T(1,128)S(1)}, u32[]{:S(2)}, u32[]{:S(2)}) collective-permute-start(f32[1,5120]{1,0:T(1,128)S(1)} %bitcast.136), channel_id=1, source_target_pairs={{0,2},{1,3},{2,0},{3,1},{4,6},{5,7},{6,4},{7,5},{8,10},{9,11},{10,... | collective-permute-start | bytes 61448 | tf_op jit(solution)/shard_map/ppermute | solution.py:36
  239.8 27.1 %collective-permute-start.25 = (bf16[64,5120]{1,0:T(8,128)(2,1)S(1)}, bf16[64,5120]{1,0:T(8,128)(2,1)S(1)}, u32[]{:S(2)}, u32[]{:S(2)}) collective-permute-start(bf16[64,5120]{1,0:T(8,128)(2,1)S(1)} %collective-permute-done.17), channel_id=1, source_target_pairs={{16,17},{17,18},{18,19},{19,16},{20,21},{21,22},{22,23},{23,20},{2... | collective-permute-start | bytes 1966088 | tf_op jit(solution)/shard_map/ppermute | solution.py:38
  252.4 28.5 %collective-permute-start.28 = (bf16[64,5120]{1,0:T(8,128)(2,1)S(1)}, bf16[64,5120]{1,0:T(8,128)(2,1)S(1)}, u32[]{:S(2)}, u32[]{:S(2)}) collective-permute-start(bf16[64,5120]{1,0:T(8,128)(2,1)S(1)} %collective-permute-done.26), channel_id=1, source_target_pairs={{0,1},{1,2},{2,3},{3,0},{4,5},{5,6},{6,7},{7,4},{8,9},{9,10},{10,1... | collective-permute-start | bytes 1966088 | tf_op jit(solution)/shard_map/ppermute | solution.py:36
  266.9 28.1 %collective-permute-start.27 = (bf16[64,5120]{1,0:T(8,128)(2,1)S(1)}, bf16[64,5120]{1,0:T(8,128)(2,1)S(1)}, u32[]{:S(2)}, u32[]{:S(2)}) collective-permute-start(bf16[64,5120]{1,0:T(8,128)(2,1)S(1)} %collective-permute-done.25), channel_id=1, source_target_pairs={{16,17},{17,18},{18,19},{19,16},{20,21},{21,22},{22,23},{23,20},{2... | collective-permute-start | bytes 1966088 | tf_op jit(solution)/shard_map/ppermute | solution.py:38
  280.9 25.7 %collective-permute-start.29 = (bf16[64,5120]{1,0:T(8,128)(2,1)S(1)}, bf16[64,5120]{1,0:T(8,128)(2,1)S(1)}, u32[]{:S(2)}, u32[]{:S(2)}) collective-permute-start(bf16[64,5120]{1,0:T(8,128)(2,1)S(1)} %collective-permute-done.28), channel_id=1, source_target_pairs={{0,1},{1,2},{2,3},{3,0},{4,5},{5,6},{6,7},{7,4},{8,9},{9,10},{10,1... | collective-permute-start | bytes 1966088 | tf_op jit(solution)/shard_map/ppermute | solution.py:36
  (45 other events, 320.9 us)
